TPU v7x, 32 devices: a whole 2x2x4 slice. The times are simulated.
32 devices in a mesh: dp: 8 (over z, x), owner: 4 (over y, core).
Axes of the slice: x: 2, y: 2, z: 4, core: 2. Of those that a mesh axis runs over, the one named last changes fastest.
Arguments:
- hidden: bfloat16 [8192, 6912], P(('dp', 'owner')), may hold values from -6 to 6
- grad_out: bfloat16 [8192, 2560], P(('dp', 'owner')), may hold values from -6 to 6
- block_list: int32 [128, 2], replicated, may hold values from 0 to 107, as said below
- live_block_count: int32 [32], replicated, may hold values from 1 to 4, as said below
- master: float32 [128, 4096], P(('dp', 'owner')), may hold values from -6 to 6
- moment: float32 [128, 4096], P(('dp', 'owner')), may hold values from -6 to 6
- variance: float32 [128, 4096], P(('dp', 'owner')), may hold values from 0.25 to 4
Outputs:
- new_master: float32 [128, 4096], P(('dp', 'owner'))
- new_moment: float32 [128, 4096], P(('dp', 'owner'))
- new_variance: float32 [128, 4096], P(('dp', 'owner'))
- clipped_grad: float32 [128, 4096], P(('dp', 'owner'))
- published: bfloat16 [128, 4096], replicated
Inputs may be any that keep to these rules, and one draw needn't show every extreme that they name: `block_list`: each row names a block: its row index below 108, its column index below 40; all rows name different blocks. Rows 4 o to 4 o + 3 are owner o's slots; owner o is the device whose index along dp is o // 4 and whose index along the mesh axis `owner` is o mod 4. Owner o's first live_block_count[o] slots are live, the rest padding; some owner's slots are all live.
All inputs are finite; a program needn't handle non-finite values.
Results may differ from a plain program's by a relative error of at most 0.001.
Values may be sent and summed in bfloat16 or wider, within the bound.
No kernel may reach another device: no remote copies, remote signals or barrier semaphores. Data moves between devices by JAX's collectives and lax.ppermute only.
A program may use at most 128 MiB of HBM per device.

v0:
```python
import functools
import math

import jax
import jax.numpy as jnp
from jax import lax
from jax.experimental import pallas as pl
from jax.experimental.pallas import tpu as pltpu
from jax.sharding import Mesh
from jax.sharding import PartitionSpec as P

SIDE = 64
LANES = 128
SLOTS = 4
PAIRS = SLOTS // 2
BLOCK = SIDE * SIDE
TILES = BLOCK // LANES
LOW_OCTAVE = -36
LARGEST = 6.0
SMALLEST = 1e-30
CODE_BITS = 13
EXP_ROWS = 8
GRAD_PARTS = 4
HIDDEN_PARTS = 8
CORES = 2
HALVES = 2
AXES = ("half", "chip", "core")
CHIPS = ("chip", "half")
INV_LN2 = 1.4426950408889634


def block_products(core, blocks_ref, hidden_ref, turned_ref, out_ref):
    low_lane = lax.broadcasted_iota(jnp.int32, (SIDE, LANES), 1) < SIDE

    chips = out_ref.shape[0] // HALVES

    def one_chip(peer, carry):
        owner = ((peer % HALVES) * chips + peer // HALVES) * CORES + core
        for pair in range(PAIRS):
            lefts, rights, rows = [], [], []
            for k in range(2):
                slot = owner * SLOTS + pair * 2 + k
                r = blocks_ref[0, slot]
                c = blocks_ref[1, slot]
                lefts.append(turned_ref[pl.ds(pl.multiple_of(c * SIDE, SIDE), SIDE), :])
                lanes = pl.ds(pl.multiple_of((r // 2) * LANES, LANES), LANES)
                rights.append(hidden_ref[:, lanes])
                rows.append(r)
            product = jnp.dot(
                jnp.concatenate(lefts, axis=0),
                jnp.concatenate(rights, axis=1),
                preferred_element_type=jnp.float32,
            )
            first = pltpu.roll(product[:SIDE, :LANES], (rows[0] % 2) * SIDE, 1)
            second = pltpu.roll(product[SIDE:, LANES:], ((rows[1] + 1) % 2) * SIDE, 1)
            out_ref[peer, pl.ds(pair * SIDE, SIDE), :] = jnp.where(low_lane, first, second)
        return carry

    lax.fori_loop(0, out_ref.shape[0], one_chip, 0, unroll=16)


def partner_terms_kernel(
    blocks_hbm, hidden_hbm, grad_hbm, master_hbm, moment_hbm, variance_hbm,
    out_ref, hidden_ref, turned_ref, state_ref, blocks_ref, grad_ref, sems,
):
    copies = [pltpu.make_async_copy(blocks_hbm, blocks_ref, sems.at[0])]
    for source, target, parts in ((grad_hbm, grad_ref, GRAD_PARTS), (hidden_hbm, hidden_ref, HIDDEN_PARTS)):
        step = source.shape[0] // parts
        for k in range(parts):
            rows = pl.ds(k * step, step)
            copies.append(
                pltpu.make_async_copy(source.at[rows], target.at[rows], sems.at[len(copies)])
            )
    for k, source in enumerate((master_hbm, moment_hbm, variance_hbm)):
        copies.append(pltpu.make_async_copy(source, state_ref.at[k], sems.at[len(copies)]))
    for copy in copies:
        copy.start()
    grad_end = 1 + GRAD_PARTS
    hidden_end = grad_end + HIDDEN_PARTS
    for copy in copies[:grad_end]:
        copy.wait()
    for k in range(grad_ref.shape[1] // LANES):
        turned_ref[pl.ds(k * LANES, LANES), :] = grad_ref[:, pl.ds(k * LANES, LANES)].T
    for copy in copies[grad_end:hidden_end]:
        copy.wait()
    block_products(1 - lax.axis_index("core"), blocks_ref, hidden_ref, turned_ref, out_ref)
    for copy in copies[hidden_end:]:
        copy.wait()


def own_terms_kernel(
    blocks_ref, live_ref, hidden_ref, turned_ref, out_ref, live_rows_ref
):
    block_products(lax.axis_index("core"), blocks_ref, hidden_ref, turned_ref, out_ref)
    total = live_ref[0]
    for owner in range(1, live_ref.shape[0]):
        total = total + live_ref[owner]
    owners = live_ref.shape[0] // HALVES
    me = lax.axis_index(AXES[1:])
    for half in range(HALVES):
        live = live_ref[half * owners + me]
        live_rows_ref[half] = jnp.full((8, LANES), live, jnp.int32)
    live_rows_ref[HALVES] = jnp.full((8, LANES), total, jnp.int32)


def code_kernel(per_octave, own_ref, other_ref, out_ref):
    def encode(value):
        octave = jnp.log(jnp.maximum(jnp.abs(value), 2.0**LOW_OCTAVE)) * INV_LN2
        code = (octave - LOW_OCTAVE) * per_octave
        return jnp.round(jnp.where(value < 0, -code, code)).astype(jnp.int32)

    def one_chip(chip, carry):
        code = []
        for pair in range(PAIRS):
            rows = pl.ds(pair * SIDE, SIDE)
            code.append(encode(own_ref[chip, rows, :] + other_ref[chip, rows, :]))
        out_ref[chip] = (code[0] << 16) | (code[1] & 0xFFFF)
        return carry

    lax.fori_loop(0, out_ref.shape[0], one_chip, 0, unroll=2)


def half_sum_kernel(per_octave, after_ref, recv_ref, code_ref):
    def decode(code):
        value = code.astype(jnp.float32)
        size = jnp.exp2(jnp.abs(value) * (1.0 / per_octave) + LOW_OCTAVE)
        return jnp.where(code > 0, size, jnp.where(code < 0, -size, 0.0))

    def add(offset, d, totals):
        word = recv_ref[d * HALVES + offset]
        return totals[0] + decode(word >> 16), totals[1] + decode((word << 16) >> 16)

    zero = jnp.zeros((SIDE, LANES), jnp.float32)
    chips = recv_ref.shape[0] // HALVES
    for offset in range(HALVES):
        totals = lax.fori_loop(
            0, chips, functools.partial(add, offset), (zero, zero), unroll=4
        )
        peak = jnp.max(jnp.maximum(*map(jnp.abs, totals)), axis=0, keepdims=True)
        exponent = jnp.floor(jnp.log(jnp.maximum(peak, SMALLEST)) * INV_LN2)
        scale = jnp.exp2(CODE_BITS - exponent)
        high, low = (jnp.round(total * scale).astype(jnp.int32) for total in totals)
        code_ref[offset, pl.ds(0, SIDE), :] = (high << 16) | (low & 0xFFFF)
        code_ref[offset, pl.ds(SIDE, EXP_ROWS), :] = jnp.broadcast_to(
            exponent.astype(jnp.int32), (EXP_ROWS, LANES)
        )


def sum_kernel(live_ref, own_ref, arrived_ref, grad_ref, square_ref, turned_ref):
    slot = lax.broadcasted_iota(jnp.int32, (SIDE, LANES), 1) // SIDE
    low_lane = lax.broadcasted_iota(jnp.int32, (TILES, LANES), 1) < SIDE

    def decode(code_ref, half):
        word = code_ref[half, pl.ds(0, SIDE), :]
        exponent = code_ref[half, pl.ds(SIDE, EXP_ROWS), :][:1].astype(jnp.float32)
        scale = jnp.exp2(exponent - CODE_BITS)
        return [code.astype(jnp.float32) * scale for code in (word >> 16, (word << 16) >> 16)]

    square = jnp.zeros((SIDE, LANES), jnp.float32)
    for half in range(HALVES):
        live = live_ref[half, 0:1, :]
        own, arrived = decode(own_ref, half), decode(arrived_ref, half)
        for pair in range(PAIRS):
            total = jnp.where(slot + pair * 2 < live, own[pair] + arrived[pair], 0.0)
            square = square + total * total
            turned = total.T
            turned_ref[half, pair] = jnp.concatenate([turned, turned], axis=1)
        for s in range(SLOTS):
            base = (s % 2) * SIDE
            even = turned_ref[half, s // 2, pl.ds(base, TILES, stride=2), :]
            odd = turned_ref[half, s // 2, pl.ds(base + 1, TILES, stride=2), :]
            grad_ref[half, pl.ds(s, TILES, stride=SLOTS), :] = jnp.where(low_lane, even, odd)
    square = jnp.sum(square, axis=0, keepdims=True)
    square_ref[...] = jnp.broadcast_to(square[None], square_ref.shape)


def update_kernel(
    live_ref, square_ref, grad_ref, state_ref, other_state_ref,
    spread_ref, new_master_ref, new_moment_ref, new_variance_ref, clipped_ref, rows_ref,
):
    square = square_ref[0]
    for owner in range(1, square_ref.shape[0]):
        square = square + square_ref[owner]
    square = jnp.sum(square, axis=1, keepdims=True)
    entries = live_ref[HALVES, 0:1, :].astype(jnp.float32) * BLOCK
    clip = jnp.minimum(1.0, 1.0 / jnp.sqrt(square / entries + 1e-06))
    half = lax.axis_index("half")

    def step(grad, state):
        clipped = clip * grad
        master, moment, variance = state
        moment = 0.9 * moment + 0.1 * clipped
        variance = 0.95 * variance + 0.05 * clipped * clipped
        moment_hat = moment / (1.0 - 0.9**20)
        variance_hat = variance / (1.0 - 0.95**20)
        change = moment_hat / (jnp.sqrt(variance_hat) + 1e-08) + 0.1 * master
        return master - 0.02 * change, moment, variance, clipped

    for t in range(TILES):
        lanes = pl.ds(t * LANES, LANES)
        rows = pl.ds(t * SLOTS, SLOTS)
        master, moment, variance, clipped = step(
            grad_ref[half, rows, :], [state_ref[k, :, lanes] for k in range(3)]
        )
        clipped_ref[:, lanes] = clipped
        new_moment_ref[:, lanes] = moment
        new_variance_ref[:, lanes] = variance
        new_master_ref[:, lanes] = master
        rows_ref[:, lanes] = step(
            grad_ref[1 - half, rows, :], [other_state_ref[k, :, lanes] for k in range(3)]
        )[0]
    own = new_master_ref[...].astype(jnp.bfloat16)
    other = rows_ref[...].astype(jnp.bfloat16)
    for chip in range(spread_ref.shape[0]):
        spread_ref[chip, half] = own
        spread_ref[chip, 1 - half] = other


def store_kernel(after_ref, *refs):
    half = len(refs) // 2
    for source, target in zip(refs[:half], refs[half:]):
        target[...] = source[...]


def publish_kernel(mine_ref, other_ref, out_ref):
    rows = CORES * SLOTS
    chips = mine_ref.shape[0]
    core = lax.axis_index("core")

    def weave(first_ref, second_ref):
        for half in range(HALVES):
            for chip in range(0, chips, 2):
                parts = []
                for k in range(2):
                    parts.append(first_ref[chip + k, half])
                    parts.append(second_ref[chip + k, half])
                block = jnp.concatenate(parts, axis=0)
                out_ref[pl.ds((half * chips + chip) * rows, 2 * rows), :] = block

    @pl.when(core == 0)
    def _():
        weave(mine_ref, other_ref)

    @pl.when(core == 1)
    def _():
        weave(other_ref, mine_ref)


VMEM = pl.BlockSpec(memory_space=pltpu.VMEM)
SMEM = pl.BlockSpec(memory_space=pltpu.SMEM)
ANY = pl.BlockSpec(memory_space=pl.ANY)
PARAMS = pltpu.CompilerParams(vmem_limit_bytes=40 * 1024 * 1024)


def local(hidden, grad_out, block_list, live_block_count, master, moment, variance):
    chips = lax.axis_size(CHIPS)
    tokens = hidden.shape[0]
    swap = [(0, 1), (1, 0)]
    shape = jax.ShapeDtypeStruct(master.shape, jnp.float32)
    kept = pltpu.VMEM(master.shape, jnp.float32)
    blocks = block_list.T
    top_octave = math.log2(CORES * tokens * LARGEST * LARGEST) + 0.05
    per_octave = 32767 / (top_octave - LOW_OCTAVE)
    cost = pl.CostEstimate(
        flops=2 * chips * SLOTS * SIDE * LANES * tokens,
        bytes_accessed=2 * (hidden.size + grad_out.size),
        transcendentals=0,
    )
    terms = pltpu.VMEM((chips, PAIRS * SIDE, LANES), jnp.float32)
    partner_terms, hidden, turned, state = pl.pallas_call(
        partner_terms_kernel,
        out_shape=(
            terms,
            pltpu.VMEM(hidden.shape, hidden.dtype),
            pltpu.VMEM(grad_out.shape[::-1], grad_out.dtype),
            pltpu.VMEM((3,) + master.shape, jnp.float32),
        ),
        in_specs=[ANY] * 6,
        out_specs=(VMEM,) * 4,
        scratch_shapes=[
            pltpu.SMEM(blocks.shape, jnp.int32),
            pltpu.VMEM(grad_out.shape, grad_out.dtype),
            pltpu.SemaphoreType.DMA((4 + GRAD_PARTS + HIDDEN_PARTS,)),
        ],
        compiler_params=PARAMS,
        cost_estimate=cost,
        name="partner_terms",
    )(
        *(
            pltpu.with_memory_space_constraint(x, pltpu.HBM)
            for x in (blocks, hidden, grad_out, master, moment, variance)
        )
    )
    arrived = lax.ppermute(partner_terms, "core", swap)
    other_state = lax.ppermute(state, "half", swap)
    own_terms, live_rows = pl.pallas_call(
        own_terms_kernel,
        out_shape=(terms, pltpu.VMEM((HALVES + 1, 8, LANES), jnp.int32)),
        in_specs=[SMEM, SMEM, VMEM, VMEM],
        out_specs=(VMEM, VMEM),
        compiler_params=PARAMS,
        cost_estimate=cost,
        name="own_terms",
    )(blocks, live_block_count, hidden, turned)
    codes = pl.pallas_call(
        functools.partial(code_kernel, per_octave),
        out_shape=pltpu.VMEM((chips, SIDE, LANES), jnp.int32),
        in_specs=[VMEM, VMEM],
        out_specs=VMEM,
        compiler_params=PARAMS,
        name="code_terms",
    )(own_terms, arrived)
    received = lax.cond(
        live_block_count[0] > 0,
        lambda x: lax.all_to_all(x, "chip", split_axis=0, concat_axis=0, tiled=True),
        lambda x: x,
        codes,
    )
    sum_codes = pl.pallas_call(
        functools.partial(half_sum_kernel, per_octave),
        out_shape=pltpu.VMEM((HALVES, SIDE + EXP_ROWS, LANES), jnp.int32),
        in_specs=[ANY, VMEM],
        out_specs=VMEM,
        compiler_params=PARAMS,
        name="sum_half",
    )(other_state, received)
    arrived = lax.ppermute(sum_codes, "half", swap)
    gradient, square = pl.pallas_call(
        sum_kernel,
        out_shape=(
            pltpu.VMEM((HALVES, TILES * SLOTS, LANES), jnp.float32),
            pltpu.VMEM((chips * CORES // HALVES, 1, LANES), jnp.float32),
        ),
        in_specs=[VMEM] * 3,
        out_specs=(VMEM, VMEM),
        scratch_shapes=[pltpu.VMEM((HALVES, PAIRS, LANES, LANES), jnp.float32)],
        compiler_params=PARAMS,
        name="sum_pair",
    )(live_rows, sum_codes, arrived)
    square = lax.all_to_all(square, ("core", "chip"), split_axis=0, concat_axis=0, tiled=True)
    spread, *updated = pl.pallas_call(
        update_kernel,
        out_shape=(
            pltpu.VMEM((chips // HALVES, HALVES) + master.shape, jnp.bfloat16),
            kept,
            kept,
            kept,
            kept,
        ),
        in_specs=[VMEM] * 5,
        out_specs=(VMEM,) * 5,
        scratch_shapes=[pltpu.VMEM(master.shape, jnp.float32)],
        compiler_params=PARAMS,
        name="adamw",
    )(live_rows, square, gradient, state, other_state)
    mine = lax.all_to_all(spread, "chip", split_axis=0, concat_axis=0, tiled=True)
    other = lax.ppermute(mine, "core", swap)
    results = pl.pallas_call(
        store_kernel,
        out_shape=(shape,) * 4,
        in_specs=[ANY] + [VMEM] * 4,
        out_specs=(VMEM,) * 4,
        compiler_params=PARAMS,
        name="store_state",
    )(mine, *updated)
    published = pl.pallas_call(
        publish_kernel,
        out_shape=jax.ShapeDtypeStruct((chips * CORES * SLOTS, BLOCK), jnp.bfloat16),
        in_specs=[VMEM, VMEM],
        out_specs=VMEM,
        compiler_params=PARAMS,
        name="publish",
    )(mine, other)
    return (*results, published)


def solution(mesh):
    devices = mesh.devices.reshape(HALVES, -1, CORES)
    rows = P(AXES, None)
    return jax.shard_map(
        local,
        mesh=Mesh(devices, AXES),
        in_specs=(rows, rows, P(), P(), rows, rows, rows),
        out_specs=(rows, rows, rows, rows, P()),
        check_vma=False,
    )
```

profile of v0, /device:TPU:0, one launch (start us, length us, event | category | flops | bytes accessed | tf_op | source)
XLA Modules:
  0.0 56.4 jit_solution(4887871676732221243)
XLA Ops:
  0.6 0.0 copy-start
  0.6 0.0 copy-start.1
  0.7 3.7 %partner_terms.1 = (f32[16,128,128]{2,1,0:T(8,128)S(1)}, bf16[256,6912]{1,0:T(8,128)(2,1)S(1)}, bf16[2560,256]{1,0:T(8,128)(2,1)S(1)}, f32[3,4,4096]{2,1,0:T(4,128)S(1)}) custom-call(s32[2,128]{1,0:T(2,128)} %bitcast.3, bf16[256,6912]{1,0:T(8,128)(2,1)} %hidden_hbm.1, bf16[256,2560]{1,0:T(8,128)(2,1)} %grad_hbm.1, f32[4,4096]{1,0:T(4,128)} %master_hbm.1, ...), custom_call_target="tpu_custom_call" | custom-call | flops 268435456 | bytes 4849664 | tf_op jit(solution)/shard_map/partner_terms/pallas_call | solution.py:270
  4.3 0.5 collective-permute-start.1
  4.8 3.7 %collective-permute-start = (f32[3,4,4096]{2,1,0:T(4,128)S(1)}, f32[3,4,4096]{2,1,0:T(4,128)S(1)}, u32[]{:S(2)}, u32[]{:S(2)}) collective-permute-start(f32[3,4,4096]{2,1,0:T(4,128)S(1)} %get-tuple-element.30.state_ref), channel_id=1, source_target_pairs={{0,16},{16,0},{1,17},{17,1},{2,18},{18,2},{3,19},{19,3},{4,20},{20... | collective-permute-start | bytes 589832 | tf_op jit(solution)/shard_map/ppermute | solution.py:295
  8.5 0.0 copy-done.1
  8.5 0.0 copy-done
  8.6 1.7 %own_terms.1 = (f32[16,128,128]{2,1,0:T(8,128)S(1)}, s32[3,8,128]{2,1,0:T(8,128)S(1)}) custom-call(s32[2,128]{1,0:T(2,128)S(1)} %bitcast.4, s32[32]{0:T(128)S(1)} %copy-done.1, bf16[256,6912]{1,0:T(8,128)(2,1)S(1)} %get-tuple-element.27.hidden_ref, bf16[2560,256]{1,0:T(8,128)(2,1)S(1)} %get-tuple-element.28.turned_ref), custom_call_target="tpu_custom_call" | custom-call | flops 268435456 | bytes 4849664 | tf_op jit(solution)/shard_map/own_terms/pallas_call | solution.py:296
  10.3 0.0 collective-permute-done.1.other_ref
  10.3 0.6 %code_terms.1 = s32[16,64,128]{2,1,0:T(8,128)S(1)} custom-call(f32[16,128,128]{2,1,0:T(8,128)S(1)} %get-tuple-element.31.own_ref, f32[16,128,128]{2,1,0:T(8,128)S(1)} %collective-permute-done.1.other_ref), custom_call_target="tpu_custom_call" | custom-call | tf_op jit(solution)/shard_map/code_terms/pallas_call | solution.py:305
  10.9 14.6 %conditional.1 = (s32[16,64,128]{2,1,0:T(8,128)S(1)}) conditional(s32[]{:T(128)} %bitcast.1, s32[16,64,128]{2,1,0:T(8,128)S(1)} %code_terms.1, s32[16,64,128]{2,1,0:T(8,128)S(1)} %code_terms.1), branch_computations={%region_0.0_spmd, %region_1.0_spmd} | conditional | bytes 2097160 | solution.py:313
  10.9 14.5 %all_to_all.14 = s32[16,64,128]{2,1,0:T(8,128)S(1)} all-to-all(s32[16,64,128]{2,1,0:T(8,128)S(1)} %copy.14), channel_id=1, replica_groups=mesh['half'=2,'chip'=8,'core'=2] {'chip'}, dimensions={0} | all-to-all | bytes 1048576 | tf_op jit(solution)/shard_map/cond/branch_1_fun/all_to_all | solution.py:315
  25.4 0.0 collective-permute-done.after_ref.other_state_ref
  25.4 0.5 sum_half.1.own_ref
  25.9 0.6 %collective-permute-start.2 = (s32[2,72,128]{2,1,0:T(8,128)S(1)}, s32[2,72,128]{2,1,0:T(8,128)S(1)}, u32[]{:S(2)}, u32[]{:S(2)}) collective-permute-start(s32[2,72,128]{2,1,0:T(8,128)S(1)} %sum_half.1.own_ref), channel_id=1, source_target_pairs={{0,16},{16,0},{1,17},{17,1},{2,18},{18,2},{3,19},{19,3},{4,20},{20... | collective-permute-start | bytes 221192 | tf_op jit(solution)/shard_map/ppermute | solution.py:327
  26.6 5.8 %collective-permute-done.2.arrived_ref = s32[2,72,128]{2,1,0:T(8,128)S(1)} collective-permute-done((s32[2,72,128]{2,1,0:T(8,128)S(1)}, s32[2,72,128]{2,1,0:T(8,128)S(1)}, u32[]{:S(2)}, u32[]{:S(2)}) %collective-permute-start.2) | collective-permute-done | bytes 73760 | tf_op jit(solution)/shard_map/ppermute | solution.py:327
  32.4 0.3 sum_pair.1
  32.7 8.0 %all_to_all.15.square_ref = f32[16,1,128]{2,1,0:T(1,128)S(1)} all-to-all(f32[16,1,128]{2,1,0:T(1,128)S(1)} %get-tuple-element.33), channel_id=1, replica_groups=mesh['half'=2,'chip'=8,'core'=2] {'core','chip'}, dimensions={0} | all-to-all | bytes 16384 | tf_op jit(solution)/shard_map/all_to_all | solution.py:340
  40.7 0.4 adamw.1
  41.0 12.1 %all_to_all.16.after_ref.mine_ref = bf16[8,2,4,4096]{3,2,1,0:T(4,128)(2,1)S(1)} all-to-all(bf16[8,2,4,4096]{3,2,1,0:T(4,128)(2,1)S(1)} %get-tuple-element.35), channel_id=1, replica_groups=mesh['half'=2,'chip'=8,'core'=2] {'chip'}, dimensions={0} | all-to-all | bytes 1048576 | tf_op jit(solution)/shard_map/all_to_all | solution.py:356
  53.2 0.0 collective-permute-start.3
  53.2 0.7 %store_state.1 = (f32[4,4096]{1,0:T(4,128)}, f32[4,4096]{1,0:T(4,128)}, f32[4,4096]{1,0:T(4,128)}, f32[4,4096]{1,0:T(4,128)}) custom-call(bf16[8,2,4,4096]{3,2,1,0:T(4,128)(2,1)S(1)} %all_to_all.16.after_ref.mine_ref, f32[4,4096]{1,0:T(4,128)S(1)} %get-tuple-element.36.refs_0_, f32[4,4096]{1,0:T(4,128)S(1)} %get-tuple-element.37.refs_1_, ...), custom_call_target="tpu_custom_call" | custom-call | tf_op jit(solution)/shard_map/store_state/pallas_call | solution.py:358
  53.9 1.2 %collective-permute-done.3.other_ref = bf16[8,2,4,4096]{3,2,1,0:T(4,128)(2,1)S(1)} collective-permute-done((bf16[8,2,4,4096]{3,2,1,0:T(4,128)(2,1)S(1)}, bf16[8,2,4,4096]{3,2,1,0:T(4,128)(2,1)S(1)}, u32[]{:S(2)}, u32[]{:S(2)}) %collective-permute-start.3) | collective-permute-done | bytes 524320 | tf_op jit(solution)/shard_map/ppermute | solution.py:357
  55.1 1.3 %publish.1 = bf16[128,4096]{1,0:T(8,128)(2,1)} custom-call(bf16[8,2,4,4096]{3,2,1,0:T(4,128)(2,1)S(1)} %all_to_all.16.after_ref.mine_ref, bf16[8,2,4,4096]{3,2,1,0:T(4,128)(2,1)S(1)} %collective-permute-done.3.other_ref), custom_call_target="tpu_custom_call" | custom-call | tf_op jit(solution)/shard_map/publish/pallas_call | solution.py:366
  (1 shorter events, 0.0 us)
Async XLA Ops:
  0.6 7.9 %copy-start = (s32[128,2]{0,1:T(2,128)S(1)}, s32[128,2]{0,1:T(2,128)}, u32[]{:S(2)}) copy-start(s32[128,2]{0,1:T(2,128)} %param.11) | copy-start | bytes 3076
  0.6 7.9 %copy-start.1 = (s32[32]{0:T(128)S(1)}, s32[32]{0:T(128)}, u32[]{:S(2)}) copy-start(s32[32]{0:T(128)} %live_ref.1) | copy-start | bytes 388
  4.3 6.0 %collective-permute-start.1 = (f32[16,128,128]{2,1,0:T(8,128)S(1)}, f32[16,128,128]{2,1,0:T(8,128)S(1)}, u32[]{:S(2)}, u32[]{:S(2)}) collective-permute-start(f32[16,128,128]{2,1,0:T(8,128)S(1)} %get-tuple-element.32), channel_id=1, source_target_pairs={{0,1},{1,0},{2,3},{3,2},{4,5},{5,4},{6,7},{7,6},{8,9},{9,8},{10,11... | collective-permute-start | bytes 3145736 | tf_op jit(solution)/shard_map/ppermute | solution.py:294
  4.8 20.6 %collective-permute-start = (f32[3,4,4096]{2,1,0:T(4,128)S(1)}, f32[3,4,4096]{2,1,0:T(4,128)S(1)}, u32[]{:S(2)}, u32[]{:S(2)}) collective-permute-start(f32[3,4,4096]{2,1,0:T(4,128)S(1)} %get-tuple-element.30.state_ref), channel_id=1, source_target_pairs={{0,16},{16,0},{1,17},{17,1},{2,18},{18,2},{3,19},{19,3},{4,20},{20... | collective-permute-start | bytes 589832 | tf_op jit(solution)/shard_map/ppermute | solution.py:295
  25.9 6.4 %collective-permute-start.2 = (s32[2,72,128]{2,1,0:T(8,128)S(1)}, s32[2,72,128]{2,1,0:T(8,128)S(1)}, u32[]{:S(2)}, u32[]{:S(2)}) collective-permute-start(s32[2,72,128]{2,1,0:T(8,128)S(1)} %sum_half.1.own_ref), channel_id=1, source_target_pairs={{0,16},{16,0},{1,17},{17,1},{2,18},{18,2},{3,19},{19,3},{4,20},{20... | collective-permute-start | bytes 221192 | tf_op jit(solution)/shard_map/ppermute | solution.py:327
  53.2 1.9 %collective-permute-start.3 = (bf16[8,2,4,4096]{3,2,1,0:T(4,128)(2,1)S(1)}, bf16[8,2,4,4096]{3,2,1,0:T(4,128)(2,1)S(1)}, u32[]{:S(2)}, u32[]{:S(2)}) collective-permute-start(bf16[8,2,4,4096]{3,2,1,0:T(4,128)(2,1)S(1)} %all_to_all.16.after_ref.mine_ref), channel_id=1, source_target_pairs={{0,1},{1,0},{2,3},{3,2},{4,5},{5,4},{6,7},{7,6},{8,9},{9,8},{10,11... | collective-permute-start | bytes 1572872 | tf_op jit(solution)/shard_map/ppermute | solution.py:357
where the time goes:
time: 56.6 us; the launch traced here: 56.4 us
  blocking collectives  34.6 us (61%)
  Pallas kernels  9.08 us (16%)
  waiting for transfers between devices  7.05 us (12%)
  starting transfers between devices  4.8 us (8%)
  between operations  0.76 us (1%)
    all_to_all x1, blocking collectives, local(): lax.all_to_all(x, 'chip', split_axis=0, concat_axis=0, tiled=True)  14.5 us
    all_to_all x1, blocking collectives, local(): lax.all_to_all(spread, 'chip', split_axis=0, concat_axis=0, tiled=True)  12.1 us
    all_to_all x1, blocking collectives, local(): lax.all_to_all(square, ('core', 'chip'), split_axis=0, concat_axis=0, til...  8 us
    ppermute x1, waiting for transfers between devices, local(): arrived = lax.ppermute(sum_codes, 'half', swap)  5.83 us
    ppermute x1, starting transfers between devices, local(): other_state = lax.ppermute(state, 'half', swap)  3.66 us
    pallas_call x1, Pallas kernels, local(): pl.pallas_call(partner_terms_kernel, out_shape=(terms, pltpu.VMEM(hidden....  3.65 us
    pallas_call x1, Pallas kernels, local(): pl.pallas_call(own_terms_kernel, out_shape=(terms, pltpu.VMEM((HALVES + 1...  1.71 us
    pallas_call x1, Pallas kernels, local(): pl.pallas_call(publish_kernel, out_shape=jax.ShapeDtypeStruct((chips * CO...  1.29 us
  transfers between devices with their start and end apart: 4, of which 2 were waited for; matrix products, arithmetic and copies ran while one was open for 0% of the time, Pallas kernels for 5%

commit v1 on v0

--- a/solution.py
+++ b/solution.py
@@ -20,10 +20,12 @@
 SMALLEST = 1e-30
 CODE_BITS = 13
 EXP_ROWS = 8
-GRAD_PARTS = 4
-HIDDEN_PARTS = 8
+GRAD_PARTS = 8
+HIDDEN_PARTS = 16
+STORE_PARTS = 4
 CORES = 2
 HALVES = 2
+SWAP = [(0, 1), (1, 0)]
 AXES = ("half", "chip", "core")
 CHIPS = ("chip", "half")
 INV_LN2 = 1.4426950408889634
@@ -59,9 +61,19 @@
     lax.fori_loop(0, out_ref.shape[0], one_chip, 0, unroll=16)
 
 
+def gather_kernel(master_hbm, moment_hbm, variance_hbm, state_ref, sems):
+    copies = [
+        pltpu.make_async_copy(source, state_ref.at[k], sems.at[k])
+        for k, source in enumerate((master_hbm, moment_hbm, variance_hbm))
+    ]
+    for copy in copies:
+        copy.start()
+    for copy in copies:
+        copy.wait()
+
+
 def partner_terms_kernel(
-    blocks_hbm, hidden_hbm, grad_hbm, master_hbm, moment_hbm, variance_hbm,
-    out_ref, hidden_ref, turned_ref, state_ref, blocks_ref, grad_ref, sems,
+    blocks_hbm, hidden_hbm, grad_hbm, out_ref, hidden_ref, turned_ref, blocks_ref, grad_ref, sems
 ):
     copies = [pltpu.make_async_copy(blocks_hbm, blocks_ref, sems.at[0])]
     for source, target, parts in ((grad_hbm, grad_ref, GRAD_PARTS), (hidden_hbm, hidden_ref, HIDDEN_PARTS)):
@@ -71,21 +83,16 @@
             copies.append(
                 pltpu.make_async_copy(source.at[rows], target.at[rows], sems.at[len(copies)])
             )
-    for k, source in enumerate((master_hbm, moment_hbm, variance_hbm)):
-        copies.append(pltpu.make_async_copy(source, state_ref.at[k], sems.at[len(copies)]))
     for copy in copies:
         copy.start()
     grad_end = 1 + GRAD_PARTS
-    hidden_end = grad_end + HIDDEN_PARTS
     for copy in copies[:grad_end]:
         copy.wait()
     for k in range(grad_ref.shape[1] // LANES):
         turned_ref[pl.ds(k * LANES, LANES), :] = grad_ref[:, pl.ds(k * LANES, LANES)].T
-    for copy in copies[grad_end:hidden_end]:
+    for copy in copies[grad_end:]:
         copy.wait()
     block_products(1 - lax.axis_index("core"), blocks_ref, hidden_ref, turned_ref, out_ref)
-    for copy in copies[hidden_end:]:
-        copy.wait()
 
 
 def own_terms_kernel(
@@ -222,20 +229,33 @@
         target[...] = source[...]
 
 
-def publish_kernel(mine_ref, other_ref, out_ref):
+def publish_kernel(mine_ref, other_ref, out_hbm, woven_ref, sems):
     rows = CORES * SLOTS
     chips = mine_ref.shape[0]
+    parts = sems.shape[0] // HALVES
+    step = chips // parts
     core = lax.axis_index("core")
 
     def weave(first_ref, second_ref):
+        copies = []
         for half in range(HALVES):
-            for chip in range(0, chips, 2):
-                parts = []
-                for k in range(2):
-                    parts.append(first_ref[chip + k, half])
-                    parts.append(second_ref[chip + k, half])
-                block = jnp.concatenate(parts, axis=0)
-                out_ref[pl.ds((half * chips + chip) * rows, 2 * rows), :] = block
+            for part in range(parts):
+                for chip in range(part * step, (part + 1) * step, 2):
+                    pieces = []
+                    for k in range(2):
+                        pieces.append(first_ref[chip + k, half])
+                        pieces.append(second_ref[chip + k, half])
+                    block = jnp.concatenate(pieces, axis=0)
+                    woven_ref[pl.ds((half * chips + chip) * rows, 2 * rows), :] = block
+                span = pl.ds((half * chips + part * step) * rows, step * rows)
+                copies.append(
+                    pltpu.make_async_copy(
+                        woven_ref.at[span], out_hbm.at[span], sems.at[len(copies)]
+                    )
+                )
+                copies[-1].start()
+        for copy in copies:
+            copy.wait()
 
     @pl.when(core == 0)
     def _():
@@ -252,13 +272,9 @@
 PARAMS = pltpu.CompilerParams(vmem_limit_bytes=40 * 1024 * 1024)
 
 
-def local(hidden, grad_out, block_list, live_block_count, master, moment, variance):
+def exchange_terms(hidden, grad_out, blocks, live_block_count):
     chips = lax.axis_size(CHIPS)
     tokens = hidden.shape[0]
-    swap = [(0, 1), (1, 0)]
-    shape = jax.ShapeDtypeStruct(master.shape, jnp.float32)
-    kept = pltpu.VMEM(master.shape, jnp.float32)
-    blocks = block_list.T
     top_octave = math.log2(CORES * tokens * LARGEST * LARGEST) + 0.05
     per_octave = 32767 / (top_octave - LOW_OCTAVE)
     cost = pl.CostEstimate(
@@ -267,32 +283,25 @@
         transcendentals=0,
     )
     terms = pltpu.VMEM((chips, PAIRS * SIDE, LANES), jnp.float32)
-    partner_terms, hidden, turned, state = pl.pallas_call(
+    partner_terms, hidden, turned = pl.pallas_call(
         partner_terms_kernel,
         out_shape=(
             terms,
             pltpu.VMEM(hidden.shape, hidden.dtype),
             pltpu.VMEM(grad_out.shape[::-1], grad_out.dtype),
-            pltpu.VMEM((3,) + master.shape, jnp.float32),
         ),
-        in_specs=[ANY] * 6,
-        out_specs=(VMEM,) * 4,
+        in_specs=[ANY] * 3,
+        out_specs=(VMEM,) * 3,
         scratch_shapes=[
             pltpu.SMEM(blocks.shape, jnp.int32),
             pltpu.VMEM(grad_out.shape, grad_out.dtype),
-            pltpu.SemaphoreType.DMA((4 + GRAD_PARTS + HIDDEN_PARTS,)),
+            pltpu.SemaphoreType.DMA((1 + GRAD_PARTS + HIDDEN_PARTS,)),
         ],
         compiler_params=PARAMS,
         cost_estimate=cost,
         name="partner_terms",
-    )(
-        *(
-            pltpu.with_memory_space_constraint(x, pltpu.HBM)
-            for x in (blocks, hidden, grad_out, master, moment, variance)
-        )
-    )
-    arrived = lax.ppermute(partner_terms, "core", swap)
-    other_state = lax.ppermute(state, "half", swap)
+    )(*(pltpu.with_memory_space_constraint(x, pltpu.HBM) for x in (blocks, hidden, grad_out)))
+    arrived = lax.ppermute(partner_terms, "core", SWAP)
     own_terms, live_rows = pl.pallas_call(
         own_terms_kernel,
         out_shape=(terms, pltpu.VMEM((HALVES + 1, 8, LANES), jnp.int32)),
@@ -310,11 +319,41 @@
         compiler_params=PARAMS,
         name="code_terms",
     )(own_terms, arrived)
-    received = lax.cond(
+    return lax.all_to_all(codes, "chip", split_axis=0, concat_axis=0, tiled=True), live_rows
+
+
+def no_terms(hidden, grad_out, blocks, live_block_count):
+    chips = lax.axis_size(CHIPS)
+    return (
+        jnp.zeros((chips, SIDE, LANES), jnp.int32),
+        jnp.zeros((HALVES + 1, 8, LANES), jnp.int32),
+    )
+
+
+def local(hidden, grad_out, block_list, live_block_count, master, moment, variance):
+    chips = lax.axis_size(CHIPS)
+    shape = jax.ShapeDtypeStruct(master.shape, jnp.float32)
+    kept = pltpu.VMEM(master.shape, jnp.float32)
+    top_octave = math.log2(CORES * hidden.shape[0] * LARGEST * LARGEST) + 0.05
+    per_octave = 32767 / (top_octave - LOW_OCTAVE)
+    state = pl.pallas_call(
+        gather_kernel,
+        out_shape=pltpu.VMEM((3,) + master.shape, jnp.float32),
+        in_specs=[ANY] * 3,
+        out_specs=VMEM,
+        scratch_shapes=[pltpu.SemaphoreType.DMA((3,))],
+        compiler_params=PARAMS,
+        name="gather_state",
+    )(*(pltpu.with_memory_space_constraint(x, pltpu.HBM) for x in (master, moment, variance)))
+    other_state = lax.ppermute(state, "half", SWAP)
+    received, live_rows = lax.cond(
         live_block_count[0] > 0,
-        lambda x: lax.all_to_all(x, "chip", split_axis=0, concat_axis=0, tiled=True),
-        lambda x: x,
-        codes,
+        exchange_terms,
+        no_terms,
+        hidden,
+        grad_out,
+        block_list.T,
+        live_block_count,
     )
     sum_codes = pl.pallas_call(
         functools.partial(half_sum_kernel, per_octave),
@@ -324,7 +363,7 @@
         compiler_params=PARAMS,
         name="sum_half",
     )(other_state, received)
-    arrived = lax.ppermute(sum_codes, "half", swap)
+    arrived = lax.ppermute(sum_codes, "half", SWAP)
     gradient, square = pl.pallas_call(
         sum_kernel,
         out_shape=(
@@ -354,7 +393,7 @@
         name="adamw",
     )(live_rows, square, gradient, state, other_state)
     mine = lax.all_to_all(spread, "chip", split_axis=0, concat_axis=0, tiled=True)
-    other = lax.ppermute(mine, "core", swap)
+    other = lax.ppermute(mine, "core", SWAP)
     results = pl.pallas_call(
         store_kernel,
         out_shape=(shape,) * 4,
@@ -367,7 +406,11 @@
         publish_kernel,
         out_shape=jax.ShapeDtypeStruct((chips * CORES * SLOTS, BLOCK), jnp.bfloat16),
         in_specs=[VMEM, VMEM],
-        out_specs=VMEM,
+        out_specs=ANY,
+        scratch_shapes=[
+            pltpu.VMEM((chips * CORES * SLOTS, BLOCK), jnp.bfloat16),
+            pltpu.SemaphoreType.DMA((STORE_PARTS,)),
+        ],
         compiler_params=PARAMS,
         name="publish",
     )(mine, other)

time: 56.6 us -> 58.5 us (1.034)
  Pallas kernels: 9.08 us -> 9.91 us
  waiting for transfers between devices: 7.05 us -> 7.88 us
    pallas_call x3 -> x4, Pallas kernels: 5.93 us -> 6.98 us  [the longest x1 3.84 us: exchange_terms(): pl.pallas_call(partner_terms_kernel, out_shape=(terms, pltpu.VMEM(hidden....]
    ppermute x4, waiting for transfers between devices: 7.05 us -> 7.88 us  [the longest x1 5.71 us: local(): arrived = lax.ppermute(sum_codes, 'half', SWAP)]
  transfers between devices with their start and end apart: 4 -> 4, of which waited for: 2 -> 3; matrix products, arithmetic and copies ran while one was open for 0% -> 0% of each run, Pallas kernels for 5% -> 12%
where the time goes in v1:
time: 58.5 us; the launch traced here: 58.1 us
  blocking collectives  34.4 us (59%)
  Pallas kernels  9.91 us (17%)
  waiting for transfers between devices  7.88 us (13%)
  starting transfers between devices  4.57 us (8%)
  between operations  1.32 us (2%)
    all_to_all x1, blocking collectives, exchange_terms(): lax.all_to_all(codes, 'chip', split_axis=0, concat_axis=0, tiled=True)  14.3 us
    all_to_all x1, blocking collectives, local(): lax.all_to_all(spread, 'chip', split_axis=0, concat_axis=0, tiled=True)  12.1 us
    all_to_all x1, blocking collectives, local(): lax.all_to_all(square, ('core', 'chip'), split_axis=0, concat_axis=0, til...  8 us
    ppermute x1, waiting for transfers between devices, local(): arrived = lax.ppermute(sum_codes, 'half', SWAP)  5.71 us
    ppermute x1, starting transfers between devices, local(): other_state = lax.ppermute(state, 'half', SWAP)  4.1 us
    pallas_call x1, Pallas kernels, exchange_terms(): pl.pallas_call(partner_terms_kernel, out_shape=(terms, pltpu.VMEM(hidden....  3.84 us
    pallas_call x1, Pallas kernels, exchange_terms(): pl.pallas_call(own_terms_kernel, out_shape=(terms, pltpu.VMEM((HALVES + 1...  1.66 us
    ppermute x1, waiting for transfers between devices, local(): other = lax.ppermute(mine, 'core', SWAP)  1.21 us
  transfers between devices with their start and end apart: 4, of which 3 were waited for; matrix products, arithmetic and copies ran while one was open for 0% of the time, Pallas kernels for 12%

profile of v1, /device:TPU:0, one launch (start us, length us, event | category | flops | bytes accessed | tf_op | source)
XLA Modules:
  0.0 58.1 jit_solution(17547097708470963374)
XLA Ops:
  0.6 0.9 %gather_state.1.state_ref = f32[3,4,4096]{2,1,0:T(4,128)S(1)} custom-call(f32[4,4096]{1,0:T(4,128)} %master_hbm.1, f32[4,4096]{1,0:T(4,128)} %moment_hbm.1, f32[4,4096]{1,0:T(4,128)} %variance_hbm.1), custom_call_target="tpu_custom_call" | custom-call | tf_op jit(solution)/shard_map/gather_state/pallas_call | solution.py:339
  1.6 4.1 %collective-permute-start.1 = (f32[3,4,4096]{2,1,0:T(4,128)S(1)}, f32[3,4,4096]{2,1,0:T(4,128)S(1)}, u32[]{:S(2)}, u32[]{:S(2)}) collective-permute-start(f32[3,4,4096]{2,1,0:T(4,128)S(1)} %gather_state.1.state_ref), channel_id=1, source_target_pairs={{0,16},{16,0},{1,17},{17,1},{2,18},{18,2},{3,19},{19,3},{4,20},{20... | collective-permute-start | bytes 589832 | tf_op jit(solution)/shard_map/ppermute | solution.py:348
  6.3 21.4 %conditional.1 = (s32[16,64,128]{2,1,0:T(8,128)S(1)}, s32[3,8,128]{2,1,0:T(8,128)S(1)}) conditional(s32[]{:T(128)} %bitcast, () %tuple.16, (s32[2,128]{1,0:T(2,128)}, bf16[256,6912]{1,0:T(8,128)(2,1)}, bf16[256,2560]{1,0:T(8,128)(2,1)}, s32[32]{0:T(128)}) %tuple.21), branch_computations={%region_0.0_spmd, %region_1.0_spmd} | conditional | flops 536870912 | bytes 14946928 | solution.py:349
  6.3 0.0 copy-start
  6.4 0.0 copy-start.1
  6.4 3.8 %partner_terms.1 = (f32[16,128,128]{2,1,0:T(8,128)S(1)}, bf16[256,6912]{1,0:T(8,128)(2,1)S(1)}, bf16[2560,256]{1,0:T(8,128)(2,1)S(1)}) custom-call(s32[2,128]{1,0:T(2,128)} %get-tuple-element.8.blocks_hbm.blocks_ref, bf16[256,6912]{1,0:T(8,128)(2,1)} %get-tuple-element.50.hidden_hbm, bf16[256,2560]{1,0:T(8,128)(2,1)} %get-tuple-element.51.grad_hbm), custom_call_target="tpu_custom_call" | custom-call | flops 268435456 | bytes 4849664 | tf_op jit(solution)/shard_map/cond/branch_1_fun/partner_terms/pallas_call | solution.py:286
  10.2 0.1 collective-permute-start
  10.3 0.0 copy-done
  10.3 0.0 copy-done.1
  10.3 1.7 %own_terms.1 = (f32[16,128,128]{2,1,0:T(8,128)S(1)}, s32[3,8,128]{2,1,0:T(8,128)S(1)}) custom-call(s32[2,128]{1,0:T(2,128)S(1)} %copy-done, s32[32]{0:T(128)S(1)} %copy-done.1, bf16[256,6912]{1,0:T(8,128)(2,1)S(1)} %get-tuple-element.12.hidden_ref, bf16[2560,256]{1,0:T(8,128)(2,1)S(1)} %get-tuple-element.13.turned_ref), custom_call_target="tpu_custom_call" | custom-call | flops 268435456 | bytes 4849664 | tf_op jit(solution)/shard_map/cond/branch_1_fun/own_terms/pallas_call | solution.py:305
  12.0 1.0 %collective-permute-done.other_ref = f32[16,128,128]{2,1,0:T(8,128)S(1)} collective-permute-done((f32[16,128,128]{2,1,0:T(8,128)S(1)}, f32[16,128,128]{2,1,0:T(8,128)S(1)}, u32[]{:S(2)}, u32[]{:S(2)}) %collective-permute-start) | collective-permute-done | bytes 1048608 | tf_op jit(solution)/shard_map/cond/branch_1_fun/ppermute | solution.py:304
  12.9 0.5 code_terms.1
  13.5 14.3 %all_to_all.14 = s32[16,64,128]{2,1,0:T(8,128)S(1)} all-to-all(s32[16,64,128]{2,1,0:T(8,128)S(1)} %code_terms.1), channel_id=1, replica_groups=mesh['half'=2,'chip'=8,'core'=2] {'chip'}, dimensions={0} | all-to-all | bytes 1048576 | tf_op jit(solution)/shard_map/cond/branch_1_fun/all_to_all | solution.py:322
  27.7 0.0 collective-permute-done.1.after_ref.other_state_ref
  27.7 0.5 sum_half.1.own_ref
  28.3 0.4 collective-permute-start.2
  28.7 5.7 %collective-permute-done.2.arrived_ref = s32[2,72,128]{2,1,0:T(8,128)S(1)} collective-permute-done((s32[2,72,128]{2,1,0:T(8,128)S(1)}, s32[2,72,128]{2,1,0:T(8,128)S(1)}, u32[]{:S(2)}, u32[]{:S(2)}) %collective-permute-start.2) | collective-permute-done | bytes 73760 | tf_op jit(solution)/shard_map/ppermute | solution.py:366
  34.4 0.3 sum_pair.1
  34.6 8.0 %all_to_all.15.square_ref = f32[16,1,128]{2,1,0:T(1,128)S(1)} all-to-all(f32[16,1,128]{2,1,0:T(1,128)S(1)} %get-tuple-element.37), channel_id=1, replica_groups=mesh['half'=2,'chip'=8,'core'=2] {'core','chip'}, dimensions={0} | all-to-all | bytes 16384 | tf_op jit(solution)/shard_map/all_to_all | solution.py:379
  42.6 0.4 adamw.1
  43.0 12.1 %all_to_all.16.after_ref.mine_ref = bf16[8,2,4,4096]{3,2,1,0:T(4,128)(2,1)S(1)} all-to-all(bf16[8,2,4,4096]{3,2,1,0:T(4,128)(2,1)S(1)} %get-tuple-element.39), channel_id=1, replica_groups=mesh['half'=2,'chip'=8,'core'=2] {'chip'}, dimensions={0} | all-to-all | bytes 1048576 | tf_op jit(solution)/shard_map/all_to_all | solution.py:395
  55.2 0.0 collective-permute-start.3
  55.2 0.7 %store_state.1 = (f32[4,4096]{1,0:T(4,128)}, f32[4,4096]{1,0:T(4,128)}, f32[4,4096]{1,0:T(4,128)}, f32[4,4096]{1,0:T(4,128)}) custom-call(bf16[8,2,4,4096]{3,2,1,0:T(4,128)(2,1)S(1)} %all_to_all.16.after_ref.mine_ref, f32[4,4096]{1,0:T(4,128)S(1)} %get-tuple-element.40.refs_0_, f32[4,4096]{1,0:T(4,128)S(1)} %get-tuple-element.41.refs_1_, ...), custom_call_target="tpu_custom_call" | custom-call | tf_op jit(solution)/shard_map/store_state/pallas_call | solution.py:397
  55.9 1.2 %collective-permute-done.3.other_ref = bf16[8,2,4,4096]{3,2,1,0:T(4,128)(2,1)S(1)} collective-permute-done((bf16[8,2,4,4096]{3,2,1,0:T(4,128)(2,1)S(1)}, bf16[8,2,4,4096]{3,2,1,0:T(4,128)(2,1)S(1)}, u32[]{:S(2)}, u32[]{:S(2)}) %collective-permute-start.3) | collective-permute-done | bytes 524320 | tf_op jit(solution)/shard_map/ppermute | solution.py:396
  57.1 1.1 %publish.1 = bf16[128,4096]{1,0:T(8,128)(2,1)} custom-call(bf16[8,2,4,4096]{3,2,1,0:T(4,128)(2,1)S(1)} %all_to_all.16.after_ref.mine_ref, bf16[8,2,4,4096]{3,2,1,0:T(4,128)(2,1)S(1)} %collective-permute-done.3.other_ref), custom_call_target="tpu_custom_call" | custom-call | tf_op jit(solution)/shard_map/publish/pallas_call | solution.py:405
Async XLA Ops:
  1.6 26.2 %collective-permute-start.1 = (f32[3,4,4096]{2,1,0:T(4,128)S(1)}, f32[3,4,4096]{2,1,0:T(4,128)S(1)}, u32[]{:S(2)}, u32[]{:S(2)}) collective-permute-start(f32[3,4,4096]{2,1,0:T(4,128)S(1)} %gather_state.1.state_ref), channel_id=1, source_target_pairs={{0,16},{16,0},{1,17},{17,1},{2,18},{18,2},{3,19},{19,3},{4,20},{20... | collective-permute-start | bytes 589832 | tf_op jit(solution)/shard_map/ppermute | solution.py:348
  6.3 4.0 %copy-start = (s32[2,128]{1,0:T(2,128)S(1)}, s32[2,128]{1,0:T(2,128)}, u32[]{:S(2)}) copy-start(s32[2,128]{1,0:T(2,128)} %get-tuple-element.8.blocks_hbm.blocks_ref) | copy-start | bytes 3076 | tf_op jit(solution)/shard_map/cond
  6.4 4.0 %copy-start.1 = (s32[32]{0:T(128)S(1)}, s32[32]{0:T(128)}, u32[]{:S(2)}) copy-start(s32[32]{0:T(128)} %get-tuple-element.9.live_ref) | copy-start | bytes 388 | tf_op jit(solution)/shard_map/cond
  10.2 2.7 %collective-permute-start = (f32[16,128,128]{2,1,0:T(8,128)S(1)}, f32[16,128,128]{2,1,0:T(8,128)S(1)}, u32[]{:S(2)}, u32[]{:S(2)}) collective-permute-start(f32[16,128,128]{2,1,0:T(8,128)S(1)} %get-tuple-element.15), channel_id=1, source_target_pairs={{0,1},{1,0},{2,3},{3,2},{4,5},{5,4},{6,7},{7,6},{8,9},{9,8},{10,11... | collective-permute-start | bytes 3145736 | tf_op jit(solution)/shard_map/cond/branch_1_fun/ppermute | solution.py:304
  28.3 6.1 %collective-permute-start.2 = (s32[2,72,128]{2,1,0:T(8,128)S(1)}, s32[2,72,128]{2,1,0:T(8,128)S(1)}, u32[]{:S(2)}, u32[]{:S(2)}) collective-permute-start(s32[2,72,128]{2,1,0:T(8,128)S(1)} %sum_half.1.own_ref), channel_id=1, source_target_pairs={{0,16},{16,0},{1,17},{17,1},{2,18},{18,2},{3,19},{19,3},{4,20},{20... | collective-permute-start | bytes 221192 | tf_op jit(solution)/shard_map/ppermute | solution.py:366
  55.2 1.9 %collective-permute-start.3 = (bf16[8,2,4,4096]{3,2,1,0:T(4,128)(2,1)S(1)}, bf16[8,2,4,4096]{3,2,1,0:T(4,128)(2,1)S(1)}, u32[]{:S(2)}, u32[]{:S(2)}) collective-permute-start(bf16[8,2,4,4096]{3,2,1,0:T(4,128)(2,1)S(1)} %all_to_all.16.after_ref.mine_ref), channel_id=1, source_target_pairs={{0,1},{1,0},{2,3},{3,2},{4,5},{5,4},{6,7},{7,6},{8,9},{9,8},{10,11... | collective-permute-start | bytes 1572872 | tf_op jit(solution)/shard_map/ppermute | solution.py:396

commit v2 on v0

--- a/solution.py
+++ b/solution.py
@@ -22,6 +22,7 @@
 EXP_ROWS = 8
 GRAD_PARTS = 4
 HIDDEN_PARTS = 8
+STORE_PARTS = 4
 CORES = 2
 HALVES = 2
 AXES = ("half", "chip", "core")
@@ -89,7 +90,7 @@
 
 
 def own_terms_kernel(
-    blocks_ref, live_ref, hidden_ref, turned_ref, out_ref, live_rows_ref
+    blocks_ref, live_ref, hidden_ref, turned_ref, state_in, out_ref, live_rows_ref, state_ref
 ):
     block_products(lax.axis_index("core"), blocks_ref, hidden_ref, turned_ref, out_ref)
     total = live_ref[0]
@@ -101,6 +102,7 @@
         live = live_ref[half * owners + me]
         live_rows_ref[half] = jnp.full((8, LANES), live, jnp.int32)
     live_rows_ref[HALVES] = jnp.full((8, LANES), total, jnp.int32)
+    state_ref[...] = state_in[...]
 
 
 def code_kernel(per_octave, own_ref, other_ref, out_ref):
@@ -222,20 +224,33 @@
         target[...] = source[...]
 
 
-def publish_kernel(mine_ref, other_ref, out_ref):
+def publish_kernel(mine_ref, other_ref, out_hbm, woven_ref, sems):
     rows = CORES * SLOTS
     chips = mine_ref.shape[0]
+    parts = sems.shape[0] // HALVES
+    step = chips // parts
     core = lax.axis_index("core")
 
     def weave(first_ref, second_ref):
+        copies = []
         for half in range(HALVES):
-            for chip in range(0, chips, 2):
-                parts = []
-                for k in range(2):
-                    parts.append(first_ref[chip + k, half])
-                    parts.append(second_ref[chip + k, half])
-                block = jnp.concatenate(parts, axis=0)
-                out_ref[pl.ds((half * chips + chip) * rows, 2 * rows), :] = block
+            for part in range(parts):
+                for chip in range(part * step, (part + 1) * step, 2):
+                    pieces = []
+                    for k in range(2):
+                        pieces.append(first_ref[chip + k, half])
+                        pieces.append(second_ref[chip + k, half])
+                    block = jnp.concatenate(pieces, axis=0)
+                    woven_ref[pl.ds((half * chips + chip) * rows, 2 * rows), :] = block
+                span = pl.ds((half * chips + part * step) * rows, step * rows)
+                copies.append(
+                    pltpu.make_async_copy(
+                        woven_ref.at[span], out_hbm.at[span], sems.at[len(copies)]
+                    )
+                )
+                copies[-1].start()
+        for copy in copies:
+            copy.wait()
 
     @pl.when(core == 0)
     def _():
@@ -292,16 +307,20 @@
         )
     )
     arrived = lax.ppermute(partner_terms, "core", swap)
-    other_state = lax.ppermute(state, "half", swap)
-    own_terms, live_rows = pl.pallas_call(
+    own_terms, live_rows, state = pl.pallas_call(
         own_terms_kernel,
-        out_shape=(terms, pltpu.VMEM((HALVES + 1, 8, LANES), jnp.int32)),
-        in_specs=[SMEM, SMEM, VMEM, VMEM],
-        out_specs=(VMEM, VMEM),
+        out_shape=(
+            terms,
+            pltpu.VMEM((HALVES + 1, 8, LANES), jnp.int32),
+            pltpu.VMEM((3,) + master.shape, jnp.float32),
+        ),
+        in_specs=[SMEM, SMEM, VMEM, VMEM, VMEM],
+        out_specs=(VMEM,) * 3,
         compiler_params=PARAMS,
         cost_estimate=cost,
         name="own_terms",
-    )(blocks, live_block_count, hidden, turned)
+    )(blocks, live_block_count, hidden, turned, state)
+    other_state = lax.ppermute(state, "half", swap)
     codes = pl.pallas_call(
         functools.partial(code_kernel, per_octave),
         out_shape=pltpu.VMEM((chips, SIDE, LANES), jnp.int32),
@@ -313,7 +332,7 @@
     received = lax.cond(
         live_block_count[0] > 0,
         lambda x: lax.all_to_all(x, "chip", split_axis=0, concat_axis=0, tiled=True),
-        lambda x: x,
+        jnp.zeros_like,
         codes,
     )
     sum_codes = pl.pallas_call(
@@ -367,7 +386,11 @@
         publish_kernel,
         out_shape=jax.ShapeDtypeStruct((chips * CORES * SLOTS, BLOCK), jnp.bfloat16),
         in_specs=[VMEM, VMEM],
-        out_specs=VMEM,
+        out_specs=ANY,
+        scratch_shapes=[
+            pltpu.VMEM((chips * CORES * SLOTS, BLOCK), jnp.bfloat16),
+            pltpu.SemaphoreType.DMA((STORE_PARTS,)),
+        ],
         compiler_params=PARAMS,
         name="publish",
     )(mine, other)

time: 56.6 us -> 57.6 us (1.018)
  blocking collectives: 34.6 us -> 36.3 us
    all_to_all x1, blocking collectives: 14.5 us -> 16.1 us  [local(): lax.all_to_all(x, 'chip', split_axis=0, concat_axis=0, tiled=True)]
where the time goes in v2:
time: 57.6 us; the launch traced here: 57.4 us
  blocking collectives  36.3 us (63%)
  Pallas kernels  8.81 us (15%)
  waiting for transfers between devices  7.24 us (13%)
  starting transfers between devices  4.27 us (7%)
  between operations  0.76 us (1%)
    all_to_all x1, blocking collectives, local(): lax.all_to_all(x, 'chip', split_axis=0, concat_axis=0, tiled=True)  16.1 us
    all_to_all x1, blocking collectives, local(): lax.all_to_all(spread, 'chip', split_axis=0, concat_axis=0, tiled=True)  12.1 us
    all_to_all x1, blocking collectives, local(): lax.all_to_all(square, ('core', 'chip'), split_axis=0, concat_axis=0, til...  8.12 us
    ppermute x1, waiting for transfers between devices, local(): arrived = lax.ppermute(sum_codes, 'half', swap)  6.03 us
    ppermute x1, starting transfers between devices, local(): other_state = lax.ppermute(state, 'half', swap)  3.69 us
    pallas_call x1, Pallas kernels, local(): pl.pallas_call(partner_terms_kernel, out_shape=(terms, pltpu.VMEM(hidden....  3.66 us
    pallas_call x1, Pallas kernels, local(): pl.pallas_call(own_terms_kernel, out_shape=(terms, pltpu.VMEM((HALVES + 1...  1.64 us
    ppermute x1, waiting for transfers between devices, local(): other = lax.ppermute(mine, 'core', swap)  1.21 us
  transfers between devices with their start and end apart: 4, of which 2 were waited for; matrix products, arithmetic and copies ran while one was open for 0% of the time, Pallas kernels for 5%

profile of v2, /device:TPU:0, one launch (start us, length us, event | category | flops | bytes accessed | tf_op | source)
XLA Modules:
  0.0 57.4 jit_solution(6665593428121205830)
XLA Ops:
  0.6 0.0 copy-start
  0.6 0.0 copy-start.1
  0.7 3.7 %partner_terms.1 = (f32[16,128,128]{2,1,0:T(8,128)S(1)}, bf16[256,6912]{1,0:T(8,128)(2,1)S(1)}, bf16[2560,256]{1,0:T(8,128)(2,1)S(1)}, f32[3,4,4096]{2,1,0:T(4,128)S(1)}) custom-call(s32[2,128]{1,0:T(2,128)} %bitcast.3, bf16[256,6912]{1,0:T(8,128)(2,1)} %hidden_hbm.1, bf16[256,2560]{1,0:T(8,128)(2,1)} %grad_hbm.1, f32[4,4096]{1,0:T(4,128)} %master_hbm.1, ...), custom_call_target="tpu_custom_call" | custom-call | flops 268435456 | bytes 4849664 | tf_op jit(solution)/shard_map/partner_terms/pallas_call | solution.py:285
  4.3 0.5 collective-permute-start.1
  4.8 0.0 copy-done
  4.8 0.0 copy-done.1
  4.8 1.6 %own_terms.1 = (f32[16,128,128]{2,1,0:T(8,128)S(1)}, s32[3,8,128]{2,1,0:T(8,128)S(1)}, f32[3,4,4096]{2,1,0:T(4,128)S(1)}) custom-call(s32[2,128]{1,0:T(2,128)S(1)} %bitcast.4, s32[32]{0:T(128)S(1)} %copy-done.1, bf16[256,6912]{1,0:T(8,128)(2,1)S(1)} %get-tuple-element.27.hidden_ref, bf16[2560,256]{1,0:T(8,128)(2,1)S(1)} %get-tuple-element.28.turned_ref, ...), custom_call_target="tpu_custom_call" | custom-call | flops 268435456 | bytes 4849664 | tf_op jit(solution)/shard_map/own_terms/pallas_call | solution.py:310
  6.5 3.7 %collective-permute-start = (f32[3,4,4096]{2,1,0:T(4,128)S(1)}, f32[3,4,4096]{2,1,0:T(4,128)S(1)}, u32[]{:S(2)}, u32[]{:S(2)}) collective-permute-start(f32[3,4,4096]{2,1,0:T(4,128)S(1)} %get-tuple-element.31.state_ref), channel_id=1, source_target_pairs={{0,16},{16,0},{1,17},{17,1},{2,18},{18,2},{3,19},{19,3},{4,20},{20... | collective-permute-start | bytes 589832 | tf_op jit(solution)/shard_map/ppermute | solution.py:323
  10.2 0.0 collective-permute-done.1.other_ref
  10.2 0.6 code_terms.1
  10.8 16.1 %conditional.1 = (s32[16,64,128]{2,1,0:T(8,128)S(1)}) conditional(s32[]{:T(128)} %bitcast.1, () %tuple.14, s32[16,64,128]{2,1,0:T(8,128)S(1)} %code_terms.1), branch_computations={%region_0.0_spmd, %region_1.0_spmd} | conditional | bytes 1048584 | solution.py:332
  10.8 16.1 %all_to_all.14 = s32[16,64,128]{2,1,0:T(8,128)S(1)} all-to-all(s32[16,64,128]{2,1,0:T(8,128)S(1)} %param.1), channel_id=1, replica_groups=mesh['half'=2,'chip'=8,'core'=2] {'chip'}, dimensions={0} | all-to-all | bytes 1048576 | tf_op jit(solution)/shard_map/cond/branch_1_fun/all_to_all | solution.py:334
  26.9 0.0 collective-permute-done.after_ref.other_state_ref
  26.9 0.5 sum_half.1.own_ref
  27.4 0.1 collective-permute-start.2
  27.5 6.0 %collective-permute-done.2.arrived_ref = s32[2,72,128]{2,1,0:T(8,128)S(1)} collective-permute-done((s32[2,72,128]{2,1,0:T(8,128)S(1)}, s32[2,72,128]{2,1,0:T(8,128)S(1)}, u32[]{:S(2)}, u32[]{:S(2)}) %collective-permute-start.2) | collective-permute-done | bytes 73760 | tf_op jit(solution)/shard_map/ppermute | solution.py:346
  33.5 0.3 sum_pair.1
  33.8 8.1 %all_to_all.15.square_ref = f32[16,1,128]{2,1,0:T(1,128)S(1)} all-to-all(f32[16,1,128]{2,1,0:T(1,128)S(1)} %get-tuple-element.34), channel_id=1, replica_groups=mesh['half'=2,'chip'=8,'core'=2] {'core','chip'}, dimensions={0} | all-to-all | bytes 16384 | tf_op jit(solution)/shard_map/all_to_all | solution.py:359
  41.9 0.4 adamw.1
  42.3 12.1 %all_to_all.16.after_ref.mine_ref = bf16[8,2,4,4096]{3,2,1,0:T(4,128)(2,1)S(1)} all-to-all(bf16[8,2,4,4096]{3,2,1,0:T(4,128)(2,1)S(1)} %get-tuple-element.36), channel_id=1, replica_groups=mesh['half'=2,'chip'=8,'core'=2] {'chip'}, dimensions={0} | all-to-all | bytes 1048576 | tf_op jit(solution)/shard_map/all_to_all | solution.py:375
  54.4 0.0 collective-permute-start.3
  54.4 0.7 %store_state.1 = (f32[4,4096]{1,0:T(4,128)}, f32[4,4096]{1,0:T(4,128)}, f32[4,4096]{1,0:T(4,128)}, f32[4,4096]{1,0:T(4,128)}) custom-call(bf16[8,2,4,4096]{3,2,1,0:T(4,128)(2,1)S(1)} %all_to_all.16.after_ref.mine_ref, f32[4,4096]{1,0:T(4,128)S(1)} %get-tuple-element.37.refs_0_, f32[4,4096]{1,0:T(4,128)S(1)} %get-tuple-element.38.refs_1_, ...), custom_call_target="tpu_custom_call" | custom-call | tf_op jit(solution)/shard_map/store_state/pallas_call | solution.py:377
  55.1 1.2 %collective-permute-done.3.other_ref = bf16[8,2,4,4096]{3,2,1,0:T(4,128)(2,1)S(1)} collective-permute-done((bf16[8,2,4,4096]{3,2,1,0:T(4,128)(2,1)S(1)}, bf16[8,2,4,4096]{3,2,1,0:T(4,128)(2,1)S(1)}, u32[]{:S(2)}, u32[]{:S(2)}) %collective-permute-start.3) | collective-permute-done | bytes 524320 | tf_op jit(solution)/shard_map/ppermute | solution.py:376
  56.3 1.1 %publish.1 = bf16[128,4096]{1,0:T(8,128)(2,1)} custom-call(bf16[8,2,4,4096]{3,2,1,0:T(4,128)(2,1)S(1)} %all_to_all.16.after_ref.mine_ref, bf16[8,2,4,4096]{3,2,1,0:T(4,128)(2,1)S(1)} %collective-permute-done.3.other_ref), custom_call_target="tpu_custom_call" | custom-call | tf_op jit(solution)/shard_map/publish/pallas_call | solution.py:385
Async XLA Ops:
  0.6 4.2 %copy-start = (s32[128,2]{0,1:T(2,128)S(1)}, s32[128,2]{0,1:T(2,128)}, u32[]{:S(2)}) copy-start(s32[128,2]{0,1:T(2,128)} %param.11) | copy-start | bytes 3076
  0.6 4.2 %copy-start.1 = (s32[32]{0:T(128)S(1)}, s32[32]{0:T(128)}, u32[]{:S(2)}) copy-start(s32[32]{0:T(128)} %live_ref.1) | copy-start | bytes 388
  4.3 5.9 %collective-permute-start.1 = (f32[16,128,128]{2,1,0:T(8,128)S(1)}, f32[16,128,128]{2,1,0:T(8,128)S(1)}, u32[]{:S(2)}, u32[]{:S(2)}) collective-permute-start(f32[16,128,128]{2,1,0:T(8,128)S(1)} %get-tuple-element.33), channel_id=1, source_target_pairs={{0,1},{1,0},{2,3},{3,2},{4,5},{5,4},{6,7},{7,6},{8,9},{9,8},{10,11... | collective-permute-start | bytes 3145736 | tf_op jit(solution)/shard_map/ppermute | solution.py:309
  6.5 20.4 %collective-permute-start = (f32[3,4,4096]{2,1,0:T(4,128)S(1)}, f32[3,4,4096]{2,1,0:T(4,128)S(1)}, u32[]{:S(2)}, u32[]{:S(2)}) collective-permute-start(f32[3,4,4096]{2,1,0:T(4,128)S(1)} %get-tuple-element.31.state_ref), channel_id=1, source_target_pairs={{0,16},{16,0},{1,17},{17,1},{2,18},{18,2},{3,19},{19,3},{4,20},{20... | collective-permute-start | bytes 589832 | tf_op jit(solution)/shard_map/ppermute | solution.py:323
  27.4 6.1 %collective-permute-start.2 = (s32[2,72,128]{2,1,0:T(8,128)S(1)}, s32[2,72,128]{2,1,0:T(8,128)S(1)}, u32[]{:S(2)}, u32[]{:S(2)}) collective-permute-start(s32[2,72,128]{2,1,0:T(8,128)S(1)} %sum_half.1.own_ref), channel_id=1, source_target_pairs={{0,16},{16,0},{1,17},{17,1},{2,18},{18,2},{3,19},{19,3},{4,20},{20... | collective-permute-start | bytes 221192 | tf_op jit(solution)/shard_map/ppermute | solution.py:346
  54.4 1.9 %collective-permute-start.3 = (bf16[8,2,4,4096]{3,2,1,0:T(4,128)(2,1)S(1)}, bf16[8,2,4,4096]{3,2,1,0:T(4,128)(2,1)S(1)}, u32[]{:S(2)}, u32[]{:S(2)}) collective-permute-start(bf16[8,2,4,4096]{3,2,1,0:T(4,128)(2,1)S(1)} %all_to_all.16.after_ref.mine_ref), channel_id=1, source_target_pairs={{0,1},{1,0},{2,3},{3,2},{4,5},{5,4},{6,7},{7,6},{8,9},{9,8},{10,11... | collective-permute-start | bytes 1572872 | tf_op jit(solution)/shard_map/ppermute | solution.py:376

commit v3 on v2

--- a/solution.py
+++ b/solution.py
@@ -20,8 +20,8 @@
 SMALLEST = 1e-30
 CODE_BITS = 13
 EXP_ROWS = 8
-GRAD_PARTS = 4
-HIDDEN_PARTS = 8
+GRAD_PARTS = 2
+HIDDEN_PARTS = 4
 STORE_PARTS = 4
 CORES = 2
 HALVES = 2
@@ -90,7 +90,7 @@
 
 
 def own_terms_kernel(
-    blocks_ref, live_ref, hidden_ref, turned_ref, state_in, out_ref, live_rows_ref, state_ref
+    blocks_ref, live_ref, hidden_ref, turned_ref, out_ref, live_rows_ref
 ):
     block_products(lax.axis_index("core"), blocks_ref, hidden_ref, turned_ref, out_ref)
     total = live_ref[0]
@@ -102,7 +102,6 @@
         live = live_ref[half * owners + me]
         live_rows_ref[half] = jnp.full((8, LANES), live, jnp.int32)
     live_rows_ref[HALVES] = jnp.full((8, LANES), total, jnp.int32)
-    state_ref[...] = state_in[...]
 
 
 def code_kernel(per_octave, own_ref, other_ref, out_ref):
@@ -119,7 +118,7 @@
         out_ref[chip] = (code[0] << 16) | (code[1] & 0xFFFF)
         return carry
 
-    lax.fori_loop(0, out_ref.shape[0], one_chip, 0, unroll=2)
+    lax.fori_loop(0, out_ref.shape[0], one_chip, 0, unroll=4)
 
 
 def half_sum_kernel(per_octave, after_ref, recv_ref, code_ref):
@@ -136,7 +135,7 @@
     chips = recv_ref.shape[0] // HALVES
     for offset in range(HALVES):
         totals = lax.fori_loop(
-            0, chips, functools.partial(add, offset), (zero, zero), unroll=4
+            0, chips, functools.partial(add, offset), (zero, zero), unroll=8
         )
         peak = jnp.max(jnp.maximum(*map(jnp.abs, totals)), axis=0, keepdims=True)
         exponent = jnp.floor(jnp.log(jnp.maximum(peak, SMALLEST)) * INV_LN2)
@@ -307,20 +306,16 @@
         )
     )
     arrived = lax.ppermute(partner_terms, "core", swap)
-    own_terms, live_rows, state = pl.pallas_call(
+    other_state = lax.ppermute(state, "half", swap)
+    own_terms, live_rows = pl.pallas_call(
         own_terms_kernel,
-        out_shape=(
-            terms,
-            pltpu.VMEM((HALVES + 1, 8, LANES), jnp.int32),
-            pltpu.VMEM((3,) + master.shape, jnp.float32),
-        ),
-        in_specs=[SMEM, SMEM, VMEM, VMEM, VMEM],
-        out_specs=(VMEM,) * 3,
+        out_shape=(terms, pltpu.VMEM((HALVES + 1, 8, LANES), jnp.int32)),
+        in_specs=[SMEM, SMEM, VMEM, VMEM],
+        out_specs=(VMEM, VMEM),
         compiler_params=PARAMS,
         cost_estimate=cost,
         name="own_terms",
-    )(blocks, live_block_count, hidden, turned, state)
-    other_state = lax.ppermute(state, "half", swap)
+    )(blocks, live_block_count, hidden, turned)
     codes = pl.pallas_call(
         functools.partial(code_kernel, per_octave),
         out_shape=pltpu.VMEM((chips, SIDE, LANES), jnp.int32),

time: 57.6 us -> 56.3 us (0.977)
  blocking collectives: 36.3 us -> 34.8 us
    all_to_all x1, blocking collectives: 16.1 us -> 14.7 us  [local(): lax.all_to_all(x, 'chip', split_axis=0, concat_axis=0, tiled=True)]
where the time goes in v3:
time: 56.3 us; the launch traced here: 56.1 us
  blocking collectives  34.8 us (62%)
  Pallas kernels  8.68 us (15%)
  waiting for transfers between devices  7.16 us (13%)
  starting transfers between devices  4.67 us (8%)
  between operations  0.76 us (1%)
    all_to_all x1, blocking collectives, local(): lax.all_to_all(x, 'chip', split_axis=0, concat_axis=0, tiled=True)  14.7 us
    all_to_all x1, blocking collectives, local(): lax.all_to_all(spread, 'chip', split_axis=0, concat_axis=0, tiled=True)  12.1 us
    all_to_all x1, blocking collectives, local(): lax.all_to_all(square, ('core', 'chip'), split_axis=0, concat_axis=0, til...  8 us
    ppermute x1, waiting for transfers between devices, local(): arrived = lax.ppermute(sum_codes, 'half', swap)  5.94 us
    ppermute x1, starting transfers between devices, local(): other_state = lax.ppermute(state, 'half', swap)  3.65 us
    pallas_call x1, Pallas kernels, local(): pl.pallas_call(partner_terms_kernel, out_shape=(terms, pltpu.VMEM(hidden....  3.63 us
    pallas_call x1, Pallas kernels, local(): pl.pallas_call(own_terms_kernel, out_shape=(terms, pltpu.VMEM((HALVES + 1...  1.68 us
    ppermute x1, waiting for transfers between devices, local(): other = lax.ppermute(mine, 'core', swap)  1.21 us
  transfers between devices with their start and end apart: 4, of which 2 were waited for; matrix products, arithmetic and copies ran while one was open for 0% of the time, Pallas kernels for 5%

profile of v3, /device:TPU:0, one launch (start us, length us, event | category | flops | bytes accessed | tf_op | source)
XLA Modules:
  0.0 56.1 jit_solution(16863868238739330695)
XLA Ops:
  0.6 0.0 copy-start
  0.6 0.0 copy-start.1
  0.7 3.6 %partner_terms.1 = (f32[16,128,128]{2,1,0:T(8,128)S(1)}, bf16[256,6912]{1,0:T(8,128)(2,1)S(1)}, bf16[2560,256]{1,0:T(8,128)(2,1)S(1)}, f32[3,4,4096]{2,1,0:T(4,128)S(1)}) custom-call(s32[2,128]{1,0:T(2,128)} %bitcast.3, bf16[256,6912]{1,0:T(8,128)(2,1)} %hidden_hbm.1, bf16[256,2560]{1,0:T(8,128)(2,1)} %grad_hbm.1, f32[4,4096]{1,0:T(4,128)} %master_hbm.1, ...), custom_call_target="tpu_custom_call" | custom-call | flops 268435456 | bytes 4849664 | tf_op jit(solution)/shard_map/partner_terms/pallas_call | solution.py:284
  4.3 0.5 collective-permute-start.1
  4.8 3.6 %collective-permute-start = (f32[3,4,4096]{2,1,0:T(4,128)S(1)}, f32[3,4,4096]{2,1,0:T(4,128)S(1)}, u32[]{:S(2)}, u32[]{:S(2)}) collective-permute-start(f32[3,4,4096]{2,1,0:T(4,128)S(1)} %get-tuple-element.29.state_ref), channel_id=1, source_target_pairs={{0,16},{16,0},{1,17},{17,1},{2,18},{18,2},{3,19},{19,3},{4,20},{20... | collective-permute-start | bytes 589832 | tf_op jit(solution)/shard_map/ppermute | solution.py:309
  8.5 0.0 copy-done.1
  8.5 0.0 copy-done
  8.5 1.7 %own_terms.1 = (f32[16,128,128]{2,1,0:T(8,128)S(1)}, s32[3,8,128]{2,1,0:T(8,128)S(1)}) custom-call(s32[2,128]{1,0:T(2,128)S(1)} %bitcast.4, s32[32]{0:T(128)S(1)} %copy-done.1, bf16[256,6912]{1,0:T(8,128)(2,1)S(1)} %get-tuple-element.26.hidden_ref, bf16[2560,256]{1,0:T(8,128)(2,1)S(1)} %get-tuple-element.27.turned_ref), custom_call_target="tpu_custom_call" | custom-call | flops 268435456 | bytes 4849664 | tf_op jit(solution)/shard_map/own_terms/pallas_call | solution.py:310
  10.2 0.0 collective-permute-done.1.other_ref
  10.2 0.5 code_terms.1
  10.7 14.7 %conditional.1 = (s32[16,64,128]{2,1,0:T(8,128)S(1)}) conditional(s32[]{:T(128)} %bitcast.1, () %tuple.14, s32[16,64,128]{2,1,0:T(8,128)S(1)} %code_terms.1), branch_computations={%region_0.0_spmd, %region_1.0_spmd} | conditional | bytes 1048584 | solution.py:327
  10.7 14.7 %all_to_all.14 = s32[16,64,128]{2,1,0:T(8,128)S(1)} all-to-all(s32[16,64,128]{2,1,0:T(8,128)S(1)} %param.1), channel_id=1, replica_groups=mesh['half'=2,'chip'=8,'core'=2] {'chip'}, dimensions={0} | all-to-all | bytes 1048576 | tf_op jit(solution)/shard_map/cond/branch_1_fun/all_to_all | solution.py:329
  25.4 0.0 collective-permute-done.after_ref.other_state_ref
  25.4 0.5 sum_half.1.own_ref
  25.9 0.5 collective-permute-start.2
  26.4 5.9 %collective-permute-done.2.arrived_ref = s32[2,72,128]{2,1,0:T(8,128)S(1)} collective-permute-done((s32[2,72,128]{2,1,0:T(8,128)S(1)}, s32[2,72,128]{2,1,0:T(8,128)S(1)}, u32[]{:S(2)}, u32[]{:S(2)}) %collective-permute-start.2) | collective-permute-done | bytes 73760 | tf_op jit(solution)/shard_map/ppermute | solution.py:341
  32.3 0.3 sum_pair.1
  32.6 8.0 %all_to_all.15.square_ref = f32[16,1,128]{2,1,0:T(1,128)S(1)} all-to-all(f32[16,1,128]{2,1,0:T(1,128)S(1)} %get-tuple-element.32), channel_id=1, replica_groups=mesh['half'=2,'chip'=8,'core'=2] {'core','chip'}, dimensions={0} | all-to-all | bytes 16384 | tf_op jit(solution)/shard_map/all_to_all | solution.py:354
  40.6 0.4 adamw.1
  41.0 12.1 %all_to_all.16.after_ref.mine_ref = bf16[8,2,4,4096]{3,2,1,0:T(4,128)(2,1)S(1)} all-to-all(bf16[8,2,4,4096]{3,2,1,0:T(4,128)(2,1)S(1)} %get-tuple-element.34), channel_id=1, replica_groups=mesh['half'=2,'chip'=8,'core'=2] {'chip'}, dimensions={0} | all-to-all | bytes 1048576 | tf_op jit(solution)/shard_map/all_to_all | solution.py:370
  53.1 0.0 collective-permute-start.3
  53.1 0.7 %store_state.1 = (f32[4,4096]{1,0:T(4,128)}, f32[4,4096]{1,0:T(4,128)}, f32[4,4096]{1,0:T(4,128)}, f32[4,4096]{1,0:T(4,128)}) custom-call(bf16[8,2,4,4096]{3,2,1,0:T(4,128)(2,1)S(1)} %all_to_all.16.after_ref.mine_ref, f32[4,4096]{1,0:T(4,128)S(1)} %get-tuple-element.35.refs_0_, f32[4,4096]{1,0:T(4,128)S(1)} %get-tuple-element.36.refs_1_, ...), custom_call_target="tpu_custom_call" | custom-call | tf_op jit(solution)/shard_map/store_state/pallas_call | solution.py:372
  53.8 1.2 %collective-permute-done.3.other_ref = bf16[8,2,4,4096]{3,2,1,0:T(4,128)(2,1)S(1)} collective-permute-done((bf16[8,2,4,4096]{3,2,1,0:T(4,128)(2,1)S(1)}, bf16[8,2,4,4096]{3,2,1,0:T(4,128)(2,1)S(1)}, u32[]{:S(2)}, u32[]{:S(2)}) %collective-permute-start.3) | collective-permute-done | bytes 524320 | tf_op jit(solution)/shard_map/ppermute | solution.py:371
  55.0 1.1 %publish.1 = bf16[128,4096]{1,0:T(8,128)(2,1)} custom-call(bf16[8,2,4,4096]{3,2,1,0:T(4,128)(2,1)S(1)} %all_to_all.16.after_ref.mine_ref, bf16[8,2,4,4096]{3,2,1,0:T(4,128)(2,1)S(1)} %collective-permute-done.3.other_ref), custom_call_target="tpu_custom_call" | custom-call | tf_op jit(solution)/shard_map/publish/pallas_call | solution.py:380
Async XLA Ops:
  0.6 7.9 %copy-start = (s32[128,2]{0,1:T(2,128)S(1)}, s32[128,2]{0,1:T(2,128)}, u32[]{:S(2)}) copy-start(s32[128,2]{0,1:T(2,128)} %param.11) | copy-start | bytes 3076
  0.6 7.8 %copy-start.1 = (s32[32]{0:T(128)S(1)}, s32[32]{0:T(128)}, u32[]{:S(2)}) copy-start(s32[32]{0:T(128)} %live_ref.1) | copy-start | bytes 388
  4.3 5.9 %collective-permute-start.1 = (f32[16,128,128]{2,1,0:T(8,128)S(1)}, f32[16,128,128]{2,1,0:T(8,128)S(1)}, u32[]{:S(2)}, u32[]{:S(2)}) collective-permute-start(f32[16,128,128]{2,1,0:T(8,128)S(1)} %get-tuple-element.31), channel_id=1, source_target_pairs={{0,1},{1,0},{2,3},{3,2},{4,5},{5,4},{6,7},{7,6},{8,9},{9,8},{10,11... | collective-permute-start | bytes 3145736 | tf_op jit(solution)/shard_map/ppermute | solution.py:308
  4.8 20.6 %collective-permute-start = (f32[3,4,4096]{2,1,0:T(4,128)S(1)}, f32[3,4,4096]{2,1,0:T(4,128)S(1)}, u32[]{:S(2)}, u32[]{:S(2)}) collective-permute-start(f32[3,4,4096]{2,1,0:T(4,128)S(1)} %get-tuple-element.29.state_ref), channel_id=1, source_target_pairs={{0,16},{16,0},{1,17},{17,1},{2,18},{18,2},{3,19},{19,3},{4,20},{20... | collective-permute-start | bytes 589832 | tf_op jit(solution)/shard_map/ppermute | solution.py:309
  25.9 6.4 %collective-permute-start.2 = (s32[2,72,128]{2,1,0:T(8,128)S(1)}, s32[2,72,128]{2,1,0:T(8,128)S(1)}, u32[]{:S(2)}, u32[]{:S(2)}) collective-permute-start(s32[2,72,128]{2,1,0:T(8,128)S(1)} %sum_half.1.own_ref), channel_id=1, source_target_pairs={{0,16},{16,0},{1,17},{17,1},{2,18},{18,2},{3,19},{19,3},{4,20},{20... | collective-permute-start | bytes 221192 | tf_op jit(solution)/shard_map/ppermute | solution.py:341
  53.1 1.9 %collective-permute-start.3 = (bf16[8,2,4,4096]{3,2,1,0:T(4,128)(2,1)S(1)}, bf16[8,2,4,4096]{3,2,1,0:T(4,128)(2,1)S(1)}, u32[]{:S(2)}, u32[]{:S(2)}) collective-permute-start(bf16[8,2,4,4096]{3,2,1,0:T(4,128)(2,1)S(1)} %all_to_all.16.after_ref.mine_ref), channel_id=1, source_target_pairs={{0,1},{1,0},{2,3},{3,2},{4,5},{5,4},{6,7},{7,6},{8,9},{9,8},{10,11... | collective-permute-start | bytes 1572872 | tf_op jit(solution)/shard_map/ppermute | solution.py:371

commit v4 on v1

--- a/solution.py
+++ b/solution.py
@@ -20,8 +20,8 @@
 SMALLEST = 1e-30
 CODE_BITS = 13
 EXP_ROWS = 8
-GRAD_PARTS = 8
-HIDDEN_PARTS = 16
+GRAD_PARTS = 2
+HIDDEN_PARTS = 4
 STORE_PARTS = 4
 CORES = 2
 HALVES = 2
@@ -124,7 +124,7 @@
         out_ref[chip] = (code[0] << 16) | (code[1] & 0xFFFF)
         return carry
 
-    lax.fori_loop(0, out_ref.shape[0], one_chip, 0, unroll=2)
+    lax.fori_loop(0, out_ref.shape[0], one_chip, 0, unroll=4)
 
 
 def half_sum_kernel(per_octave, after_ref, recv_ref, code_ref):
@@ -141,7 +141,7 @@
     chips = recv_ref.shape[0] // HALVES
     for offset in range(HALVES):
         totals = lax.fori_loop(
-            0, chips, functools.partial(add, offset), (zero, zero), unroll=4
+            0, chips, functools.partial(add, offset), (zero, zero), unroll=8
         )
         peak = jnp.max(jnp.maximum(*map(jnp.abs, totals)), axis=0, keepdims=True)
         exponent = jnp.floor(jnp.log(jnp.maximum(peak, SMALLEST)) * INV_LN2)
@@ -347,7 +347,7 @@
     )(*(pltpu.with_memory_space_constraint(x, pltpu.HBM) for x in (master, moment, variance)))
     other_state = lax.ppermute(state, "half", SWAP)
     received, live_rows = lax.cond(
-        live_block_count[0] > 0,
+        lax.axis_index("chip") < lax.axis_size("chip"),
         exchange_terms,
         no_terms,
         hidden,

time: 58.5 us -> 57.4 us (0.981)
  between operations: 1.32 us -> 0.67 us
  transfers between devices with their start and end apart: 4 -> 4, of which waited for: 3 -> 3; matrix products, arithmetic and copies ran while one was open for 0% -> 0% of each run, Pallas kernels for 12% -> 11%
where the time goes in v4:
time: 57.4 us; the launch traced here: 57.1 us
  blocking collectives  34.4 us (60%)
  Pallas kernels  9.53 us (17%)
  waiting for transfers between devices  7.9 us (14%)
  starting transfers between devices  4.57 us (8%)
  between operations  0.67 us (1%)
    all_to_all x1, blocking collectives, exchange_terms(): lax.all_to_all(codes, 'chip', split_axis=0, concat_axis=0, tiled=True)  14.3 us
    all_to_all x1, blocking collectives, local(): lax.all_to_all(spread, 'chip', split_axis=0, concat_axis=0, tiled=True)  12.1 us
    all_to_all x1, blocking collectives, local(): lax.all_to_all(square, ('core', 'chip'), split_axis=0, concat_axis=0, til...  8 us
    ppermute x1, waiting for transfers between devices, local(): arrived = lax.ppermute(sum_codes, 'half', SWAP)  5.71 us
    ppermute x1, starting transfers between devices, local(): other_state = lax.ppermute(state, 'half', SWAP)  4.1 us
    pallas_call x1, Pallas kernels, exchange_terms(): pl.pallas_call(partner_terms_kernel, out_shape=(terms, pltpu.VMEM(hidden....  3.61 us
    pallas_call x1, Pallas kernels, exchange_terms(): pl.pallas_call(own_terms_kernel, out_shape=(terms, pltpu.VMEM((HALVES + 1...  1.64 us
    ppermute x1, waiting for transfers between devices, local(): other = lax.ppermute(mine, 'core', SWAP)  1.21 us
  transfers between devices with their start and end apart: 4, of which 3 were waited for; matrix products, arithmetic and copies ran while one was open for 0% of the time, Pallas kernels for 11%

profile of v4, /device:TPU:0, one launch (start us, length us, event | category | flops | bytes accessed | tf_op | source)
XLA Modules:
  0.0 57.1 jit_solution(2082464604176843644)
XLA Ops:
  0.6 0.9 %gather_state.1.state_ref = f32[3,4,4096]{2,1,0:T(4,128)S(1)} custom-call(f32[4,4096]{1,0:T(4,128)} %master_hbm.1, f32[4,4096]{1,0:T(4,128)} %moment_hbm.1, f32[4,4096]{1,0:T(4,128)} %variance_hbm.1), custom_call_target="tpu_custom_call" | custom-call | tf_op jit(solution)/shard_map/gather_state/pallas_call | solution.py:339
  1.6 4.1 %collective-permute-start.1 = (f32[3,4,4096]{2,1,0:T(4,128)S(1)}, f32[3,4,4096]{2,1,0:T(4,128)S(1)}, u32[]{:S(2)}, u32[]{:S(2)}) collective-permute-start(f32[3,4,4096]{2,1,0:T(4,128)S(1)} %gather_state.1.state_ref), channel_id=1, source_target_pairs={{0,16},{16,0},{1,17},{17,1},{2,18},{18,2},{3,19},{19,3},{4,20},{20... | collective-permute-start | bytes 589832 | tf_op jit(solution)/shard_map/ppermute | solution.py:348
  5.7 21.1 %conditional.1 = (s32[16,64,128]{2,1,0:T(8,128)S(1)}, s32[3,8,128]{2,1,0:T(8,128)S(1)}) conditional(s32[]{:T(128)} %convert_element_type.3, () %tuple.16, (s32[2,128]{1,0:T(2,128)}, bf16[256,6912]{1,0:T(8,128)(2,1)}, bf16[256,2560]{1,0:T(8,128)(2,1)}, s32[32]{0:T(128)}) %tuple.21), branch_computations={%region_0.0_spmd, %region_1.0_spmd} | conditional | flops 536870912 | bytes 14946928 | solution.py:349
  5.7 0.0 copy-start
  5.7 0.0 copy-start.1
  5.7 3.6 %partner_terms.1 = (f32[16,128,128]{2,1,0:T(8,128)S(1)}, bf16[256,6912]{1,0:T(8,128)(2,1)S(1)}, bf16[2560,256]{1,0:T(8,128)(2,1)S(1)}) custom-call(s32[2,128]{1,0:T(2,128)} %get-tuple-element.8.blocks_hbm.blocks_ref, bf16[256,6912]{1,0:T(8,128)(2,1)} %get-tuple-element.51.hidden_hbm, bf16[256,2560]{1,0:T(8,128)(2,1)} %get-tuple-element.52.grad_hbm), custom_call_target="tpu_custom_call" | custom-call | flops 268435456 | bytes 4849664 | tf_op jit(solution)/shard_map/cond/branch_1_fun/partner_terms/pallas_call | solution.py:286
  9.3 0.1 collective-permute-start
  9.4 0.0 copy-done
  9.4 0.0 copy-done.1
  9.4 1.6 %own_terms.1 = (f32[16,128,128]{2,1,0:T(8,128)S(1)}, s32[3,8,128]{2,1,0:T(8,128)S(1)}) custom-call(s32[2,128]{1,0:T(2,128)S(1)} %copy-done, s32[32]{0:T(128)S(1)} %copy-done.1, bf16[256,6912]{1,0:T(8,128)(2,1)S(1)} %get-tuple-element.12.hidden_ref, bf16[2560,256]{1,0:T(8,128)(2,1)S(1)} %get-tuple-element.13.turned_ref), custom_call_target="tpu_custom_call" | custom-call | flops 268435456 | bytes 4849664 | tf_op jit(solution)/shard_map/cond/branch_1_fun/own_terms/pallas_call | solution.py:305
  11.0 1.0 %collective-permute-done.other_ref = f32[16,128,128]{2,1,0:T(8,128)S(1)} collective-permute-done((f32[16,128,128]{2,1,0:T(8,128)S(1)}, f32[16,128,128]{2,1,0:T(8,128)S(1)}, u32[]{:S(2)}, u32[]{:S(2)}) %collective-permute-start) | collective-permute-done | bytes 1048608 | tf_op jit(solution)/shard_map/cond/branch_1_fun/ppermute | solution.py:304
  12.0 0.5 code_terms.1
  12.5 14.3 %all_to_all.14 = s32[16,64,128]{2,1,0:T(8,128)S(1)} all-to-all(s32[16,64,128]{2,1,0:T(8,128)S(1)} %code_terms.1), channel_id=1, replica_groups=mesh['half'=2,'chip'=8,'core'=2] {'chip'}, dimensions={0} | all-to-all | bytes 1048576 | tf_op jit(solution)/shard_map/cond/branch_1_fun/all_to_all | solution.py:322
  26.8 0.0 collective-permute-done.1.after_ref.other_state_ref
  26.8 0.5 sum_half.1.own_ref
  27.2 0.4 collective-permute-start.2
  27.6 5.7 %collective-permute-done.2.arrived_ref = s32[2,72,128]{2,1,0:T(8,128)S(1)} collective-permute-done((s32[2,72,128]{2,1,0:T(8,128)S(1)}, s32[2,72,128]{2,1,0:T(8,128)S(1)}, u32[]{:S(2)}, u32[]{:S(2)}) %collective-permute-start.2) | collective-permute-done | bytes 73760 | tf_op jit(solution)/shard_map/ppermute | solution.py:366
  33.3 0.3 sum_pair.1
  33.6 8.0 %all_to_all.15.square_ref = f32[16,1,128]{2,1,0:T(1,128)S(1)} all-to-all(f32[16,1,128]{2,1,0:T(1,128)S(1)} %get-tuple-element.37), channel_id=1, replica_groups=mesh['half'=2,'chip'=8,'core'=2] {'core','chip'}, dimensions={0} | all-to-all | bytes 16384 | tf_op jit(solution)/shard_map/all_to_all | solution.py:379
  41.6 0.4 adamw.1
  42.0 12.1 %all_to_all.16.after_ref.mine_ref = bf16[8,2,4,4096]{3,2,1,0:T(4,128)(2,1)S(1)} all-to-all(bf16[8,2,4,4096]{3,2,1,0:T(4,128)(2,1)S(1)} %get-tuple-element.39), channel_id=1, replica_groups=mesh['half'=2,'chip'=8,'core'=2] {'chip'}, dimensions={0} | all-to-all | bytes 1048576 | tf_op jit(solution)/shard_map/all_to_all | solution.py:395
  54.1 0.0 collective-permute-start.3
  54.1 0.7 %store_state.1 = (f32[4,4096]{1,0:T(4,128)}, f32[4,4096]{1,0:T(4,128)}, f32[4,4096]{1,0:T(4,128)}, f32[4,4096]{1,0:T(4,128)}) custom-call(bf16[8,2,4,4096]{3,2,1,0:T(4,128)(2,1)S(1)} %all_to_all.16.after_ref.mine_ref, f32[4,4096]{1,0:T(4,128)S(1)} %get-tuple-element.40.refs_0_, f32[4,4096]{1,0:T(4,128)S(1)} %get-tuple-element.41.refs_1_, ...), custom_call_target="tpu_custom_call" | custom-call | tf_op jit(solution)/shard_map/store_state/pallas_call | solution.py:397
  54.8 1.2 %collective-permute-done.3.other_ref = bf16[8,2,4,4096]{3,2,1,0:T(4,128)(2,1)S(1)} collective-permute-done((bf16[8,2,4,4096]{3,2,1,0:T(4,128)(2,1)S(1)}, bf16[8,2,4,4096]{3,2,1,0:T(4,128)(2,1)S(1)}, u32[]{:S(2)}, u32[]{:S(2)}) %collective-permute-start.3) | collective-permute-done | bytes 524320 | tf_op jit(solution)/shard_map/ppermute | solution.py:396
  56.0 1.1 %publish.1 = bf16[128,4096]{1,0:T(8,128)(2,1)} custom-call(bf16[8,2,4,4096]{3,2,1,0:T(4,128)(2,1)S(1)} %all_to_all.16.after_ref.mine_ref, bf16[8,2,4,4096]{3,2,1,0:T(4,128)(2,1)S(1)} %collective-permute-done.3.other_ref), custom_call_target="tpu_custom_call" | custom-call | tf_op jit(solution)/shard_map/publish/pallas_call | solution.py:405
Async XLA Ops:
  1.6 25.2 %collective-permute-start.1 = (f32[3,4,4096]{2,1,0:T(4,128)S(1)}, f32[3,4,4096]{2,1,0:T(4,128)S(1)}, u32[]{:S(2)}, u32[]{:S(2)}) collective-permute-start(f32[3,4,4096]{2,1,0:T(4,128)S(1)} %gather_state.1.state_ref), channel_id=1, source_target_pairs={{0,16},{16,0},{1,17},{17,1},{2,18},{18,2},{3,19},{19,3},{4,20},{20... | collective-permute-start | bytes 589832 | tf_op jit(solution)/shard_map/ppermute | solution.py:348
  5.7 3.7 %copy-start = (s32[2,128]{1,0:T(2,128)S(1)}, s32[2,128]{1,0:T(2,128)}, u32[]{:S(2)}) copy-start(s32[2,128]{1,0:T(2,128)} %get-tuple-element.8.blocks_hbm.blocks_ref) | copy-start | bytes 3076 | tf_op jit(solution)/shard_map/cond
  5.7 3.7 %copy-start.1 = (s32[32]{0:T(128)S(1)}, s32[32]{0:T(128)}, u32[]{:S(2)}) copy-start(s32[32]{0:T(128)} %get-tuple-element.53.live_ref) | copy-start | bytes 388 | tf_op jit(solution)/shard_map/cond
  9.3 2.7 %collective-permute-start = (f32[16,128,128]{2,1,0:T(8,128)S(1)}, f32[16,128,128]{2,1,0:T(8,128)S(1)}, u32[]{:S(2)}, u32[]{:S(2)}) collective-permute-start(f32[16,128,128]{2,1,0:T(8,128)S(1)} %get-tuple-element.15), channel_id=1, source_target_pairs={{0,1},{1,0},{2,3},{3,2},{4,5},{5,4},{6,7},{7,6},{8,9},{9,8},{10,11... | collective-permute-start | bytes 3145736 | tf_op jit(solution)/shard_map/cond/branch_1_fun/ppermute | solution.py:304
  27.2 6.1 %collective-permute-start.2 = (s32[2,72,128]{2,1,0:T(8,128)S(1)}, s32[2,72,128]{2,1,0:T(8,128)S(1)}, u32[]{:S(2)}, u32[]{:S(2)}) collective-permute-start(s32[2,72,128]{2,1,0:T(8,128)S(1)} %sum_half.1.own_ref), channel_id=1, source_target_pairs={{0,16},{16,0},{1,17},{17,1},{2,18},{18,2},{3,19},{19,3},{4,20},{20... | collective-permute-start | bytes 221192 | tf_op jit(solution)/shard_map/ppermute | solution.py:366
  54.1 1.9 %collective-permute-start.3 = (bf16[8,2,4,4096]{3,2,1,0:T(4,128)(2,1)S(1)}, bf16[8,2,4,4096]{3,2,1,0:T(4,128)(2,1)S(1)}, u32[]{:S(2)}, u32[]{:S(2)}) collective-permute-start(bf16[8,2,4,4096]{3,2,1,0:T(4,128)(2,1)S(1)} %all_to_all.16.after_ref.mine_ref), channel_id=1, source_target_pairs={{0,1},{1,0},{2,3},{3,2},{4,5},{5,4},{6,7},{7,6},{8,9},{9,8},{10,11... | collective-permute-start | bytes 1572872 | tf_op jit(solution)/shard_map/ppermute | solution.py:396
